TPU v7x, 32 devices: a whole 2x2x4 slice. The times are simulated.
32 devices in a mesh: blk: 4 (over y, x), dp: 8 (over z, core).
Axes of the slice: x: 2, y: 2, z: 4, core: 2. Of those that a mesh axis runs over, the one named last changes fastest.
Arguments:
- tokens: bfloat16 [64, 512, 768], P('dp', 'blk'), may hold values from -6 to 6
- cotangent: bfloat16 [64, 512, 768], P('dp', 'blk'), may hold values from -6 to 6
- lengths: int32 [64], P('dp'), may hold values from 1 to 512, as said below
- owners: int32 [8], replicated, may hold values from 0 to 7, as said below
- master: float32 [9216, 768], P('dp')
- moment_one: float32 [9216, 768], P('dp')
- moment_two: float32 [9216, 768], P('dp'), as said below
- vectors: float32 [9216], replicated
- vector_one: float32 [9216], replicated
- vector_two: float32 [9216], replicated, as said below
Outputs:
- output: bfloat16 [64, 512, 768], P('dp', 'blk')
- grad_tokens: bfloat16 [64, 512, 768], P('dp', 'blk')
- grad_norm: float32 [], replicated
- new_master: float32 [9216, 768], P('dp')
- new_moment_one: float32 [9216, 768], P('dp')
- new_moment_two: float32 [9216, 768], P('dp')
- new_vectors: float32 [9216], replicated
- new_vector_one: float32 [9216], replicated
- new_vector_two: float32 [9216], replicated
Inputs may be any that keep to these rules, and one draw needn't show every extreme that they name: `lengths`: in each aligned block of 8 passages (those of one index of dp) at least one passage has length 512. A permutation: index d of dp owns row block owners[d] of the weight table. `moment_two`: Positive. `vector_two`: Positive.
All inputs are finite; a program needn't handle non-finite values.
Results may differ from a plain program's by a relative error of at most 0.014.
Values may be sent and summed in bfloat16 or wider, within the bound.
A program may use at most 256 MiB of HBM per device.

v0:
```python
from functools import partial

import jax
import jax.numpy as jnp
from jax import lax
from jax.sharding import PartitionSpec as P

D = 768
HEADS = 12
HEAD_DIM = 64
FF = 3072
STEP = 10


beta_one = 0.5
beta_two = 0.5
learn_rate = 0.05
vector_rate = 0.3
weight_decay = 0.01
adam_eps = 1e-08
clip_norm = 1.0


def layer_norm(mixed):
    row_mean = jnp.mean(mixed, axis=-1, keepdims=True)
    centred = mixed - row_mean
    row_var = jnp.mean(centred * centred, axis=-1, keepdims=True)
    inv_std = lax.rsqrt(row_var + 1e-12)
    return (centred * inv_std, inv_std)


def norm_back(d_normed, normed, inv_std):
    first_mean = jnp.mean(d_normed, axis=-1, keepdims=True)
    second_mean = jnp.mean(d_normed * normed, axis=-1, keepdims=True)
    return inv_std * (d_normed - first_mean - normed * second_mean)


def contract_rows(left, right):
    return lax.dot_general(
        left, right, (((0,), (0,)), ((), ())), preferred_element_type=jnp.float32
    )


def contract_cols(left, right):
    return lax.dot_general(
        left, right, (((1,), (1,)), ((), ())), preferred_element_type=jnp.float32
    )


def adamw(weight, first, second, grad, decay, rate):
    new_first = beta_one * first + (1.0 - beta_one) * grad
    new_second = beta_two * second + (1.0 - beta_two) * grad * grad
    direction = (
        new_first
        / (1.0 - beta_one**STEP)
        / (jnp.sqrt(new_second / (1.0 - beta_two**STEP)) + adam_eps)
    )
    return (weight - rate * (direction + decay * weight), new_first, new_second)


def body(
    tokens,
    cotangent,
    lengths,
    owners,
    master,
    moment_one,
    moment_two,
    vectors,
    vector_one,
    vector_two,
):
    passages, span_len, _ = tokens.shape
    tok_rows = passages * span_len
    dp_count = lax.axis_size("dp")
    own_rows = master.shape[0]
    gathered = lax.all_gather(master.astype(jnp.bfloat16), "dp", axis=0, tiled=True)
    inverse = jnp.argsort(owners)
    weight_table = jnp.take(gathered.reshape(dp_count, own_rows, D), inverse, axis=0).reshape(-1, D)
    w_query = weight_table[0:D]
    w_key = weight_table[D : 2 * D]
    w_value = weight_table[2 * D : 3 * D]
    w_out = weight_table[3 * D : 4 * D]
    w_inner = weight_table[4 * D : 4 * D + FF]
    w_outer = weight_table[4 * D + FF : 4 * D + 2 * FF]
    b_query = vectors[0:D]
    b_value = vectors[D : 2 * D]
    b_out = vectors[2 * D : 3 * D]
    b_inner = vectors[3 * D : 3 * D + FF]
    b_outer = vectors[3 * D + FF : 4 * D + FF]
    gain_one = vectors[4 * D + FF : 5 * D + FF]
    shift_one = vectors[5 * D + FF : 6 * D + FF]
    gain_two = vectors[6 * D + FF : 7 * D + FF]
    shift_two = vectors[7 * D + FF : 8 * D + FF]
    token_flat = tokens.reshape(tok_rows, D)
    queries = (jnp.dot(token_flat, w_query, preferred_element_type=jnp.float32) + b_query).astype(
        jnp.bfloat16
    )
    key_rows = jnp.dot(token_flat, w_key, preferred_element_type=jnp.float32).astype(jnp.bfloat16)
    values = (jnp.dot(token_flat, w_value, preferred_element_type=jnp.float32) + b_value).astype(
        jnp.bfloat16
    )
    all_keys, all_values = (
        lax.all_gather(key_rows.reshape(passages, span_len, D), "blk", axis=1, tiled=True),
        lax.all_gather(values.reshape(passages, span_len, D), "blk", axis=1, tiled=True),
    )
    key_count = all_keys.shape[1]
    key_valid = jnp.arange(key_count)[None, :] < lengths[:, None]
    row_start = lax.axis_index("blk") * span_len
    own_valid = (row_start + jnp.arange(span_len))[None, :] < lengths[:, None]
    row_valid = own_valid.astype(jnp.float32)
    q_heads = queries.reshape(passages, span_len, HEADS, HEAD_DIM)
    k_heads = all_keys.reshape(passages, key_count, HEADS, HEAD_DIM)
    v_heads = all_values.reshape(passages, key_count, HEADS, HEAD_DIM)

    def scores_of():
        raw_scores = (
            jnp.einsum("bqhe,bkhe->bhqk", q_heads, k_heads, preferred_element_type=jnp.float32)
            * 0.125
        )
        return jnp.where(key_valid[:, None, None, :], raw_scores, -1000000000.0)

    scores = scores_of()
    score_peak = jnp.max(scores, axis=-1, keepdims=True)
    exp_total = jnp.sum(jnp.exp(scores - score_peak), axis=-1, keepdims=True)
    log_total = score_peak + jnp.log(exp_total)
    probs_low = jnp.exp(scores - log_total).astype(jnp.bfloat16)
    context = jnp.einsum("bhqk,bkhe->bqhe", probs_low, v_heads, preferred_element_type=jnp.float32)
    context = context.reshape(tok_rows, D).astype(jnp.bfloat16)
    attn_out = jnp.dot(context, w_out, preferred_element_type=jnp.float32) + b_out
    normed_one, inv_one = layer_norm(token_flat.astype(jnp.float32) + attn_out)
    hidden = normed_one * gain_one + shift_one
    hidden_low = hidden.astype(jnp.bfloat16)
    inner_pre = contract_cols(hidden_low, w_inner) + b_inner
    active, gelu_pull = jax.vjp(partial(jax.nn.gelu, approximate=False), inner_pre)
    active_low = active.astype(jnp.bfloat16)
    branch = jnp.dot(active_low, w_outer, preferred_element_type=jnp.float32) + b_outer
    normed_two, inv_two = layer_norm(hidden + branch)
    output = (normed_two * gain_two + shift_two).astype(jnp.bfloat16).reshape(passages, span_len, D)
    grad_out = cotangent.reshape(tok_rows, D).astype(jnp.float32) * row_valid.reshape(tok_rows, 1)
    d_gain_two = jnp.sum(grad_out * normed_two, axis=0)
    d_shift_two = jnp.sum(grad_out, axis=0)
    d_mixed_two = norm_back(grad_out * gain_two, normed_two, inv_two)
    d_branch = d_mixed_two.astype(jnp.bfloat16)
    d_b_outer = jnp.sum(d_branch.astype(jnp.float32), axis=0)
    d_w_outer = contract_rows(active_low, d_branch)
    d_active = contract_cols(d_branch, w_outer)
    d_inner = gelu_pull(d_active)[0].astype(jnp.bfloat16)
    d_b_inner = jnp.sum(d_inner.astype(jnp.float32), axis=0)
    d_w_inner = contract_rows(d_inner, hidden_low)
    d_hidden = d_mixed_two + jnp.dot(d_inner, w_inner, preferred_element_type=jnp.float32)
    d_gain_one = jnp.sum(d_hidden * normed_one, axis=0)
    d_shift_one = jnp.sum(d_hidden, axis=0)
    d_mixed_one = norm_back(d_hidden * gain_one, normed_one, inv_one)
    d_attn = d_mixed_one.astype(jnp.bfloat16)
    d_b_out = jnp.sum(d_attn.astype(jnp.float32), axis=0)
    d_w_out = contract_rows(context, d_attn)
    d_context = (
        contract_cols(d_attn, w_out)
        .astype(jnp.bfloat16)
        .reshape(passages, span_len, HEADS, HEAD_DIM)
    )
    attn_probs = jnp.exp(scores_of() - log_total)
    d_probs = jnp.einsum("bqhe,bkhe->bhqk", d_context, v_heads, preferred_element_type=jnp.float32)
    inner_sum = jnp.sum(attn_probs * d_probs, axis=-1, keepdims=True)
    d_scores = (attn_probs * (d_probs - inner_sum)).astype(jnp.bfloat16)
    d_queries = (
        jnp.einsum("bhqk,bkhe->bqhe", d_scores, k_heads, preferred_element_type=jnp.float32) * 0.125
    )
    d_queries = d_queries.reshape(tok_rows, D).astype(jnp.bfloat16)
    key_part = (
        jnp.einsum("bhqk,bqhe->bkhe", d_scores, q_heads, preferred_element_type=jnp.float32) * 0.125
    )
    value_part = jnp.einsum(
        "bhqk,bqhe->bkhe",
        attn_probs.astype(jnp.bfloat16),
        d_context,
        preferred_element_type=jnp.float32,
    )
    d_keys, d_values = (
        lax.psum_scatter(
            key_part.reshape(passages, key_count, D).astype(jnp.bfloat16),
            "blk",
            scatter_dimension=1,
            tiled=True,
        ).astype(jnp.float32),
        lax.psum_scatter(
            value_part.reshape(passages, key_count, D).astype(jnp.bfloat16),
            "blk",
            scatter_dimension=1,
            tiled=True,
        ).astype(jnp.float32),
    )
    d_keys = d_keys.reshape(tok_rows, D).astype(jnp.bfloat16)
    d_values = d_values.reshape(tok_rows, D).astype(jnp.bfloat16)
    d_w_query = contract_rows(token_flat, d_queries)
    d_w_key = contract_rows(token_flat, d_keys)
    d_w_value = contract_rows(token_flat, d_values)
    d_b_query = jnp.sum(d_queries.astype(jnp.float32), axis=0)
    d_b_value = jnp.sum(d_values.astype(jnp.float32), axis=0)
    d_tokens = (
        d_mixed_one
        + contract_cols(d_queries, w_query)
        + contract_cols(d_keys, w_key)
        + contract_cols(d_values, w_value)
    )
    grad_tokens = d_tokens.astype(jnp.bfloat16).reshape(passages, span_len, D)
    grad_table = jnp.concatenate(
        [d_w_query, d_w_key, d_w_value, d_w_out, d_w_inner, d_w_outer], axis=0
    )
    grad_vector = jnp.concatenate(
        [
            d_b_query,
            d_b_value,
            d_b_out,
            d_b_inner,
            d_b_outer,
            d_gain_one,
            d_shift_one,
            d_gain_two,
            d_shift_two,
        ],
        axis=0,
    )
    ordered = jnp.take(grad_table.reshape(dp_count, own_rows, D), owners, axis=0)
    own_partial = lax.psum_scatter(ordered.reshape(-1, D), "dp", scatter_dimension=0, tiled=True)
    own_block, vector_part = (
        lax.psum(own_partial.astype(jnp.bfloat16), "blk").astype(jnp.float32),
        lax.psum(grad_vector.astype(jnp.bfloat16), "blk").astype(jnp.float32),
    )
    vector_sum, squares = lax.psum((vector_part, jnp.sum(own_block * own_block)), "dp")
    grad_norm = jnp.sqrt(squares + jnp.sum(vector_sum * vector_sum))
    factor = jnp.minimum(1.0, clip_norm / (grad_norm + 1e-06))
    new_master, new_one, new_two = adamw(
        master, moment_one, moment_two, own_block * factor, weight_decay, learn_rate
    )
    new_vectors, new_vone, new_vtwo = adamw(
        vectors, vector_one, vector_two, vector_sum * factor, 0.0, vector_rate
    )
    return (
        output,
        grad_tokens,
        grad_norm,
        new_master,
        new_one,
        new_two,
        new_vectors,
        new_vone,
        new_vtwo,
    )


def solution(mesh):
    in_specs = (
        P("dp", "blk", None),
        P("dp", "blk", None),
        P("dp"),
        P(),
        P("dp", None),
        P("dp", None),
        P("dp", None),
        P(),
        P(),
        P(),
    )
    out_specs = (
        P("dp", "blk", None),
        P("dp", "blk", None),
        P(),
        P("dp", None),
        P("dp", None),
        P("dp", None),
        P(),
        P(),
        P(),
    )
    return jax.shard_map(body, mesh=mesh, in_specs=in_specs, out_specs=out_specs, check_vma=False)
```

profile of v0, /device:TPU:0, one launch (start us, length us, event | category | flops | bytes accessed | tf_op | source)
XLA Modules:
  0.0 1106.6 jit_solution(5781824951246302650)
XLA Ops:
  11.8 131.3 %all-gather.4.cloned.1.call-done = bf16[9216,768]{1,0:T(8,128)(2,1)} async-done(((bf16[1152,768]{1,0:T(8,128)(2,1)}), bf16[9216,768]{1,0:T(8,128)(2,1)}) %all-gather.4.cloned.1.call-update) | async-done | bytes 14155792 | tf_op jit(solution)/shard_map/all_gather | solution.py:77
  143.1 12.2 %gather_fusion = bf16[8,1152,768]{2,1,0:T(8,128)(2,1)} fusion(bf16[8,1152,768]{2,1,0:T(8,128)(2,1)} %bitcast.120, s32[1024]{0:T(1024)S(1)} %pad_clamp_fusion.1), kind=kCustom, calls=%fused_computation | custom fusion | bytes 28311584 | tf_op jit(solution)/shard_map/jit(_take)/gather | solution.py:79
  155.3 9.2 bitcast_select_fusion.1
  184.3 56.7 %all-gather.8.cloned.1.call-done = bf16[8,512,768]{1,0,2:T(8,128)(2,1)} async-done(((bf16[8,128,768]{1,0,2:T(8,128)(2,1)}), bf16[8,512,768]{1,0,2:T(8,128)(2,1)}) %all-gather.8.cloned.1.call-update) | async-done | bytes 6291472 | tf_op jit(solution)/shard_map/all_gather | solution.py:104
  246.0 11.8 %fusion = (f32[8,12,128]{2,1,0:T(8,128)S(1)}, f32[8,12,128,512]{3,2,1,0:T(8,128)}) fusion(pred[8,512]{1,0:T(8,128)(4,1)S(1)} %iota_compare_fusion, bf16[8,512,12,64]{1,3,2,0:T(8,128)(2,1)S(1)} %bitcast.112, bf16[8,128,12,64]{1,0,3,2:T(8,128)(2,1)S(1)} %bitcast.118), kind=kOutput, calls=%fused_computation.8 | convolution fusion | flops 824168448 | bytes 33083392 | tf_op jit(solution)/shard_map/bqhe,bkhe->bhqk/dot_general | solution.py:118
  257.8 11.5 %exponential_reduce_fusion = f32[8,12,128]{2,1,0:T(8,128)S(1)} fusion(f32[8,12,128,512]{3,2,1,0:T(8,128)} %get-tuple-element.45, f32[8,12,128]{2,1,0:T(8,128)S(1)} %get-tuple-element.44, pred[8,512]{1,0:T(8,128)(4,1)S(1)} %iota_compare_fusion), kind=kLoop, calls=%fused_computation.6 | loop fusion | flops 25153536 | bytes 25268224 | tf_op jit(solution)/shard_map/reduce_sum | solution.py:125
  269.3 44.1 %all-gather.6.cloned.1.call-done = bf16[8,512,768]{1,0,2:T(8,128)(2,1)} async-done(((bf16[8,128,768]{1,0,2:T(8,128)(2,1)}), bf16[8,512,768]{1,0,2:T(8,128)(2,1)}) %all-gather.6.cloned.1.call-update) | async-done | bytes 6291472 | tf_op jit(solution)/shard_map/all_gather | solution.py:105
  321.1 13.2 %fusion.30 = bf16[8,128,12,64]{1,3,2,0:T(8,128)(2,1)S(1)} fusion(bf16[8,512,12,64]{1,3,2,0:T(8,128)(2,1)} %bitcast.116, f32[8,12,128,512]{3,2,1,0:T(8,128)} %get-tuple-element.45, f32[8,12,128]{2,1,0:T(8,128)S(1)} %log_add_fusion, pred[8,512]{1,0:T(8,128)(4,1)S(1)} %iota_compare_fusion), kind=kOutput, calls=%fused_computation.84 | convolution fusion | flops 831258624 | bytes 33083392 | tf_op jit(solution)/shard_map/bhqk,bkhe->bqhe/dot_general | solution.py:128
  340.0 36.7 %multiply_convert_fusion.2 = (bf16[1024,3072]{1,0:T(8,128)(2,1)S(1)}, f32[1024,3072]{1,0:T(8,128)}, f32[1024,3072]{1,0:T(8,128)}) fusion(f32[3072]{0:T(1024)S(1)} %slice.55, bf16[9216,768]{1,0:T(8,128)(2,1)} %copy-done.2, f32[1024,768]{1,0:T(8,128)S(1)} %get-tuple-element.47, f32[768]{0:T(1024)S(1)} %get-tuple-element.36, f32[768]{0:T(1024)S(1)} %get-tuple-element.37, ...), kind=kOutput, calls=%fused_computation.15 | convolution fusion | flops 5043388416 | bytes 39348224 | tf_op jit(solution)/shard_map/dot_general | solution.py:45
  376.8 10.0 fusion.73
  394.5 19.4 %fusion.75 = (bf16[3072]{0:T(1024)(128)(2,1)}, bf16[1024,3072]{1,0:T(8,128)(2,1)}) fusion(f32[1024,3072]{1,0:T(8,128)} %get-tuple-element.32, bf16[9216,768]{1,0:T(8,128)(2,1)} %copy-done.2, f32[1024,768]{1,0:T(8,128)} %get-tuple-element.28, f32[1024,3072]{1,0:T(8,128)} %get-tuple-element.48, f32[3072]{0:T(1024)S(1)} %slice.55), kind=kOutput, calls=%fused_computation.146 | convolution fusion | flops 4882953216 | bytes 39340032 | tf_op jit(solution)/shard_map/dot_general | solution.py:45
  413.8 10.5 multiply_reduce_fusion.2
  436.1 23.8 %multiply_reduce_fusion = (f32[8,12,128]{2,1,0:T(8,128)S(1)}, f32[8,12,128,512]{3,2,1,0:T(8,128)}) fusion(f32[8,12,128,512]{3,2,1,0:T(8,128)} %get-tuple-element.45, f32[8,12,128]{2,1,0:T(8,128)S(1)} %copy-done.18, pred[8,512]{1,0:T(8,128)(4,1)S(1)} %copy-done.20, bf16[8,512,12,64]{1,3,2,0:T(8,128)(2,1)} %bitcast.117, bf16[8,128,12,64]{1,0,3,2:T(8,128)(2,1)S(1)} %bitcast.126), kind=kOutput, calls=%fused_computation.4 | convolution fusion | flops 836751360 | bytes 58298368 | tf_op jit(solution)/shard_map/bqhe,bkhe->bhqk/dot_general | solution.py:164
  459.9 16.9 %multiply_convert_fusion = bf16[8,12,128,512]{3,2,1,0:T(8,128)(2,1)S(1)} fusion(f32[8,12,128,512]{3,2,1,0:T(8,128)} %get-tuple-element.53, f32[8,12,128,512]{3,2,1,0:T(8,128)} %get-tuple-element.45, f32[8,12,128]{2,1,0:T(8,128)S(1)} %get-tuple-element.52, f32[8,12,128]{2,1,0:T(8,128)S(1)} %copy-done.18, pred[8,512]{1,0:T(8,128)(4,1)S(1)} %copy-done.20), kind=kLoop, calls=%fused_computation.3 | loop fusion | flops 37748736 | bytes 63016960 | tf_op jit(solution)/shard_map/convert_element_type | solution.py:166
  492.1 15.6 %convolution_convert_fusion = bf16[8,12,64,512]{3,2,1,0:T(8,128)(2,1)} fusion(bf16[8,128,12,64]{1,0,3,2:T(8,128)(2,1)} %bitcast.127, f32[8,12,128,512]{3,2,1,0:T(8,128)} %get-tuple-element.45, f32[8,12,128]{2,1,0:T(8,128)S(1)} %copy-done.18, pred[8,512]{1,0:T(8,128)(4,1)S(1)} %copy-done.20), kind=kOutput, calls=%fused_computation.45 | convolution fusion | flops 833617920 | bytes 33083392 | tf_op jit(solution)/shard_map/bhqk,bqhe->bkhe/dot_general | solution.py:174
  517.3 12.4 %fusion.74 = (bf16[12,64]{1,0:T(8,128)(2,1)S(1)}, bf16[8,128,12,64]{1,3,2,0:T(8,128)(2,1)}) fusion(bf16[8,512,12,64]{1,3,2,0:T(8,128)(2,1)} %bitcast.113, bf16[8,12,128,512]{3,2,1,0:T(8,128)(2,1)} %copy-done), kind=kOutput, calls=%fused_computation.145 | convolution fusion | flops 807664896 | bytes 20448768 | tf_op jit(solution)/shard_map/bhqk,bkhe->bqhe/dot_general | solution.py:168
  537.7 24.8 %reduce-scatter.4.cloned.1.call-done = bf16[8,128,768]{2,1,0:T(8,128)(2,1)} async-done(((bf16[8,512,768]{2,1,0:T(8,128)(2,1)}), bf16[8,128,768]{2,1,0:T(8,128)(2,1)}) %reduce-scatter.4.cloned.1.call-update) | async-done | bytes 1572880 | tf_op jit(solution)/shard_map/reduce_scatter | solution.py:181
  567.1 68.3 %reduce-scatter.6.cloned.1.call-done = bf16[8,128,768]{2,1,0:T(8,128)(2,1)} async-done(((bf16[8,512,768]{2,1,0:T(8,128)(2,1)}), bf16[8,128,768]{2,1,0:T(8,128)(2,1)}) %reduce-scatter.6.cloned.1.call-update) | async-done | bytes 1572880 | tf_op jit(solution)/shard_map/reduce_scatter | solution.py:187
  659.5 20.7 %gather_fusion.1 = f32[8,1152,768]{2,1,0:T(8,128)} fusion(f32[8,1152,768]{2,1,0:T(8,128)} %bitcast.114, s32[1024]{0:T(1024)S(1)} %pad_clamp_fusion), kind=kCustom, calls=%fused_computation.1 | custom fusion | bytes 56623136 | tf_op jit(solution)/shard_map/jit(_take)/gather | solution.py:225
  680.2 22.3 %bitcast_select_fusion = f32[9216,768]{1,0:T(8,128)} fusion(f32[8,1152,768]{2,1,0:T(8,128)} %gather_fusion.1, pred[9216]{0:T(1024)(128)(4,1)S(1)} %broadcast_in_dim.84), kind=kLoop, calls=%fused_computation.2 | loop fusion | flops 7077888 | bytes 56632320 | tf_op jit(solution)/shard_map/jit(_take)/select_n | solution.py:225
  702.6 276.9 %reduce-scatter.8.cloned.1.call-done = f32[1152,768]{1,0:T(8,128)} async-done(((f32[9216,768]{1,0:T(8,128)}), f32[1152,768]{1,0:T(8,128)}) %reduce-scatter.8.cloned.1.call-update) | async-done | bytes 3538960 | tf_op jit(solution)/shard_map/reduce_scatter | solution.py:226
  989.8 17.4 %psum.30 = bf16[9216]{0:T(1024)(128)(2,1)} all-reduce(bf16[9216]{0:T(1024)(128)(2,1)S(1)} %dynamic-update-slice.8), channel_id=1, replica_groups=mesh['blk'=4,'dp'=8] {'blk'}, use_global_device_ids=true, to_apply=%region_27.28 | all-reduce | flops 9216 | bytes 36864 | tf_op jit(solution)/shard_map/psum | solution.py:229
  1012.0 34.3 %all-reduce.3.cloned.1.call-done = bf16[1152,768]{1,0:T(8,128)(2,1)} async-done(((bf16[1152,768]{1,0:T(8,128)(2,1)}), bf16[1152,768]{1,0:T(8,128)(2,1)}) %all-reduce.3.cloned.1.call-update) | async-done | bytes 1769488 | tf_op jit(solution)/shard_map/psum | solution.py:228
  1056.6 30.1 %all-reduce = (f32[]{:T(128)}, f32[9216]{0:T(1024)}) all-reduce(f32[]{:T(128)} %fusion.15, bf16[9216]{0:T(1024)(128)(2,1)} %psum.30), channel_id=1, replica_groups=mesh['blk'=4,'dp'=8] {'dp'}, use_global_device_ids=true, to_apply=%region_17.18 | all-reduce | flops 9217 | bytes 55304 | tf_op jit(solution)/shard_map/psum | solution.py:231
  (181 shorter events, 159.1 us)
Async XLA Ops:
  7.2 135.9 %all-gather.4.cloned.1.call-start = ((), (), s32[]{:S(2)}) async-start(), calls=%async_computation.3 | async-start | bytes 15925248 | tf_op jit(solution)/shard_map/all_gather | solution.py:77
  10.6 230.3 %all-gather.8.cloned.1.call-start = ((), (), s32[]{:S(2)}) async-start(), calls=%async_computation.5 | async-start | bytes 7864320 | tf_op jit(solution)/shard_map/all_gather | solution.py:104
  155.3 14.2 %copy-start.36 = (bf16[8,128,768]{2,1,0:T(8,128)(2,1)S(1)}, bf16[8,128,768]{2,1,0:T(8,128)(2,1)}, u32[]{:S(2)}) copy-start(bf16[8,128,768]{2,1,0:T(8,128)(2,1)} %param.10) | copy-start | bytes 4718596
  172.6 140.9 %all-gather.6.cloned.1.call-start = ((), (), s32[]{:S(2)}) async-start(), calls=%async_computation.4 | async-start | bytes 7864320 | tf_op jit(solution)/shard_map/all_gather | solution.py:105
  177.8 384.7 %reduce-scatter.4.cloned.1.call-start = ((), (), s32[]{:S(2)}) async-start(), calls=%async_computation.6 | async-start | bytes 7864320 | tf_op jit(solution)/shard_map/reduce_scatter | solution.py:181
  177.9 143.2 %copy-start.19 = (pred[8,512]{1,0:T(8,128)(4,1)}, pred[8,512]{1,0:T(8,128)(4,1)S(1)}, u32[]{:S(2)}) copy-start(pred[8,512]{1,0:T(8,128)(4,1)S(1)} %iota_compare_fusion) | copy-start | bytes 12292
  184.3 61.7 %copy-start.3 = (bf16[96,8,8,128]{3,2,1,0:T(8,128)(2,1)}, bf16[96,8,8,128]{3,2,1,0:T(8,128)(2,1)S(1)}, u32[]{:S(2)}) copy-start(bf16[96,8,8,128]{3,2,1,0:T(8,128)(2,1)S(1)} %copy.45) | copy-start | bytes 4718596
  246.0 11.8 %copy-start.1 = (bf16[8,512,768]{1,2,0:T(8,128)(2,1)}, bf16[8,512,768]{1,2,0:T(8,128)(2,1)S(1)}, u32[]{:S(2)}) copy-start(bf16[8,512,768]{1,2,0:T(8,128)(2,1)S(1)} %copy.30) | copy-start | bytes 18874372
  269.3 51.8 %copy-start.17 = (f32[8,12,128]{2,1,0:T(8,128)}, f32[8,12,128]{2,1,0:T(8,128)S(1)}, u32[]{:S(2)}) copy-start(f32[8,12,128]{2,1,0:T(8,128)S(1)} %log_add_fusion) | copy-start | bytes 147460
  340.0 36.7 %copy-start.32 = (f32[768]{0:T(1024)S(1)}, f32[768]{0:T(1024)}, u32[]{:S(2)}) copy-start(f32[768]{0:T(1024)} %get-tuple-element.35) | copy-start | bytes 9220
  376.7 10.1 copy-start.40
  376.8 10.6 copy-start.23
  376.8 10.6 copy-start.24
  376.8 10.6 copy-start.26
  436.0 23.9 %copy-start.11 = (bf16[96,8,8,128]{3,2,1,0:T(8,128)(2,1)}, bf16[96,8,8,128]{3,2,1,0:T(8,128)(2,1)S(1)}, u32[]{:S(2)}) copy-start(bf16[96,8,8,128]{3,2,1,0:T(8,128)(2,1)S(1)} %copy.48) | copy-start | bytes 4718596
  459.9 16.9 %copy-start.4 = (bf16[96,8,8,128]{3,2,1,0:T(8,128)(2,1)S(1)}, bf16[96,8,8,128]{3,2,1,0:T(8,128)(2,1)}, u32[]{:S(2)}) copy-start(bf16[96,8,8,128]{3,2,1,0:T(8,128)(2,1)} %copy-done.3) | copy-start | bytes 4718596
  492.0 143.4 %reduce-scatter.6.cloned.1.call-start = ((), (), s32[]{:S(2)}) async-start(), calls=%async_computation.7 | async-start | bytes 7864320 | tf_op jit(solution)/shard_map/reduce_scatter | solution.py:187
  516.5 463.0 %reduce-scatter.8.cloned.1.call-start = ((), (), s32[]{:S(2)}) async-start(), calls=%async_computation.8 | async-start | bytes 31850496 | tf_op jit(solution)/shard_map/reduce_scatter | solution.py:226
  640.4 11.3 %slice-start = ((s8[6291456]{0:T(1024)(128)(4,1)}), s8[4194304]{0:T(1024)(128)(4,1)S(1)}, s32[]{:S(2)}) async-start(s8[6291456]{0:T(1024)(128)(4,1)} %bitcast.140), calls=%async_computation.10 | async-start | bytes 8388608
  643.3 8.5 copy-start.12
  643.3 8.5 slice-start.1
  702.5 280.6 %copy-start.16 = (bf16[8,128,12,64]{1,0,3,2:T(8,128)(2,1)S(1)}, bf16[8,128,12,64]{1,0,3,2:T(8,128)(2,1)}, u32[]{:S(2)}) copy-start(bf16[8,128,12,64]{1,0,3,2:T(8,128)(2,1)} %copy-done.15) | copy-start | bytes 4718596
  702.5 343.9 %all-reduce.3.cloned.1.call-start = ((), (), s32[]{:S(2)}) async-start(), calls=%async_computation.9 | async-start | bytes 3538944 | tf_op jit(solution)/shard_map/psum | solution.py:228
  1049.4 41.6 %copy-start.5 = (f32[1152,768]{1,0:T(8,128)S(1)}, f32[1152,768]{1,0:T(8,128)}, u32[]{:S(2)}) copy-start(f32[1152,768]{1,0:T(8,128)} %param.14) | copy-start | bytes 10616836
  (28 other events, 116.0 us)
Sparse Core Ops, SparseCore 0:
  10.8 132.3 all-gather.3
  172.7 68.2 all-gather.7
  243.4 70.0 all-gather.5
  492.2 70.2 reduce-scatter.3
  565.3 70.1 reduce-scatter.5
  702.6 276.7 reduce-scatter.7
  983.0 63.3 all-reduce.2
where the time goes:
time: 1120 us; the launch traced here: 1110 us
  waiting for transfers between devices  637 us (57%)
  matrix products  223 us (20%)
  other arithmetic  92.7 us (8%)
  local copies, waits for them, and re-layouts  89.4 us (8%)
  blocking collectives  47.5 us (4%)
  between operations  17.5 us (2%)
    reduce_scatter x1, waiting for transfers between devices, body(): lax.psum_scatter(ordered.reshape(-1, D), 'dp', scatter_dimension=0, tiled...  277 us
    all_gather x1, waiting for transfers between devices, body(): lax.all_gather(master.astype(jnp.bfloat16), 'dp', axis=0, tiled=True)  131 us
    dot_general x6, matrix products, contract_cols(): lax.dot_general(left, right, (((1,), (1,)), ((), ())), preferred_element_...  76.5 us
    reduce_scatter x1, waiting for transfers between devices, body(): lax.psum_scatter(value_part.reshape(passages, key_count, D).astype(jnp.bf...  68.3 us
    all_gather x1, waiting for transfers between devices, body(): lax.all_gather(key_rows.reshape(passages, span_len, D), 'blk', axis=1, ti...  56.7 us
    all_gather x1, waiting for transfers between devices, body(): lax.all_gather(values.reshape(passages, span_len, D), 'blk', axis=1, tile...  44.1 us
    psum x1, waiting for transfers between devices, body(): lax.psum(own_partial.astype(jnp.bfloat16), 'blk').astype(jnp.float32)  34.3 us
    dot_general x6, matrix products, contract_rows(): lax.dot_general(left, right, (((0,), (0,)), ((), ())), preferred_element_...  33 us
  transfers between devices with their start and end apart: 7, of which 7 were waited for; matrix products, arithmetic and copies ran while one was open for 9% of the time, Pallas kernels for 0%

commit v1 on v0

v1 whole, which is shorter than its diff:
```python
import functools
import math

import jax
import jax.numpy as jnp
from jax import lax
from jax.experimental import pallas as pl
from jax.experimental.pallas import tpu as pltpu
from jax.sharding import PartitionSpec as P

D = 768
HEADS = 12
HEAD_DIM = 64
FF = 3072
STEP = 10
VEC_LEN = 8 * D + FF


beta_one = 0.5
beta_two = 0.5
learn_rate = 0.05
vector_rate = 0.3
weight_decay = 0.01
adam_eps = 1e-08
clip_norm = 1.0


def norm_back(d_normed, normed, inv_std):
    first_mean = jnp.mean(d_normed, axis=-1, keepdims=True)
    second_mean = jnp.mean(d_normed * normed, axis=-1, keepdims=True)
    return inv_std * (d_normed - first_mean - normed * second_mean)


def contract_rows(left, right):
    return lax.dot_general(
        left, right, (((0,), (0,)), ((), ())), preferred_element_type=jnp.float32
    )


def contract_cols(left, right):
    return lax.dot_general(
        left, right, (((1,), (1,)), ((), ())), preferred_element_type=jnp.float32
    )


def adamw(weight, first, second, grad, decay, rate):
    new_first = beta_one * first + (1.0 - beta_one) * grad
    new_second = beta_two * second + (1.0 - beta_two) * grad * grad
    direction = (
        new_first
        / (1.0 - beta_one**STEP)
        / (jnp.sqrt(new_second / (1.0 - beta_two**STEP)) + adam_eps)
    )
    return (weight - rate * (direction + decay * weight), new_first, new_second)


MESH = pl.DeviceIdType.MESH
GRAIN = 48
OUTER_COUNTS = (8,)
BACK_COUNTS = (2, 8)
QKV_COUNTS = (6,)


def add_low(left, right):
    return (left.astype(jnp.float32) + right.astype(jnp.float32)).astype(jnp.bfloat16)


def enter_kernel(
    nz,
    full,
    owners_ref,
    tokens_ref,
    cot_ref,
    master_ref,
    lengths_ref,
    lanes_ref,
    tokens_out,
    cot_out,
    table_out,
    q_out,
    k_out,
    v_out,
    lse_out,
    ctx_out,
    normed_out,
    inv_out,
    vec_ref,
    wide,
    own_wide,
    tokens_land,
    cot_land,
    whole_out,
    quarter_out,
    ordered,
    load_sem,
    swap_sem,
    keep_sem,
    z_sem,
    one_sem,
    two_sem,
    sib_sem,
    sib_own_sem,
    out_sem,
    q_all,
    k_all,
    v_all,
    v_turned,
    lse_all,
    ctx_all,
    normed_all,
    inv_all,
    ctx_turned,
    scores,
    weights,
    work_sem,
):
    dp, blk, z, c, y, x, sibling, x_peer, y_peer = place_of()
    diagonal = (3 - blk, dp)
    passages, span = tokens_out.shape[0], tokens_ref.shape[1]
    quarter = quarter_out.shape[4]
    low_whole, low_quarter = whole_out.at[dp], quarter_out.at[dp]

    own_rows = pl.ds(pl.multiple_of(full + blk * 2 * quarter, 16), 2 * quarter)
    loads = [
        pltpu.make_async_copy(master_ref.at[own_rows], own_wide, load_sem.at[0]),
        pltpu.make_async_copy(master_ref, wide, load_sem.at[1]),
    ]
    for load in loads:
        load.start()
    own_copies = []
    for slot, (rows_in, rows_out) in enumerate(((tokens_ref, tokens_land), (cot_ref, cot_land))):
        own_copies.append(
            pltpu.make_async_copy(
                rows_in.at[pl.ds(blk * passages, passages)],
                rows_out.at[:, pl.ds(blk * span, span)],
                keep_sem.at[slot],
            )
        )
        own_copies[-1].start()

    for row in range(VEC_LEN // D):
        for col in range(D // 128):
            at = row * (D // 128) + col
            vec_ref[row : row + 1, col * 128 : (col + 1) * 128] = lanes_ref[at : at + 1]

    barrier = pltpu.get_barrier_semaphore()
    for partner in (sibling, x_peer, y_peer, diagonal):
        pl.semaphore_signal(barrier, inc=1, device_id=partner, device_id_type=MESH)
    below, above = z > 0, z < nz - 1

    @pl.when(below)
    def _():
        pl.semaphore_signal(barrier, inc=1, device_id=(blk, dp - 2), device_id_type=MESH)

    @pl.when(above)
    def _():
        pl.semaphore_signal(barrier, inc=1, device_id=(blk, dp + 2), device_id_type=MESH)

    pl.semaphore_wait(barrier, 4 + jnp.where(below, 1, 0) + jnp.where(above, 1, 0))

    def remote(src, dst, sems, slot, device):
        return pltpu.make_async_remote_copy(
            src_ref=src,
            dst_ref=dst,
            send_sem=sems.at[(0, *slot)],
            recv_sem=sems.at[(1, *slot)],
            device_id=device,
            device_id_type=MESH,
        )

    def swap(which, rows_in, rows_out, peer, slot):
        return remote(
            rows_in.at[pl.ds(peer[0] * passages, passages)],
            rows_out.at[:, pl.ds(blk * span, span)],
            swap_sem,
            (which, slot),
            peer,
        )

    swaps = [
        swap(which, rows_in, rows_out, peer, slot)
        for which, (rows_in, rows_out) in enumerate(((tokens_ref, tokens_land), (cot_ref, cot_land)))
        for slot, peer in enumerate((x_peer, y_peer, diagonal))
    ]
    loads[0].wait()
    for half in range(2):
        quarter_out[dp, y, x, half] = own_wide[half * quarter : (half + 1) * quarter].astype(
            jnp.bfloat16
        )

    def pass_on(src_quarter, src_whole, at, upward, which):
        device = (blk, dp + 2 if upward else dp - 2)
        way = 0 if upward else 1
        if which == 0:
            return remote(src_quarter, quarter_out.at[at, y, x], z_sem, (way, 0, at // 2), device)
        return remote(src_whole, whole_out.at[at], z_sem, (way, 1, at // 2), device)

    @pl.when(above)
    def _():
        pass_on(low_quarter.at[y, x], None, dp, True, 0).start()

    @pl.when(below)
    def _():
        pass_on(low_quarter.at[y, x], None, dp, False, 0).start()

    for copy in swaps[:3]:
        copy.start()
    loads[1].wait()
    whole_out[dp] = wide[0:full].astype(jnp.bfloat16)
    for part in range(8):

        @pl.when(blk != part // 2)
        def _(part=part):
            start = full + part * quarter
            quarter_out[dp, part // 4, part // 2 % 2, part % 2] = wide[
                start : start + quarter
            ].astype(jnp.bfloat16)

    def own_whole(turn):
        @pl.when(jnp.logical_and(above, z + 1 == turn))
        def _():
            pass_on(None, low_whole, dp, True, 1).start()

        @pl.when(jnp.logical_and(below, nz - z == turn))
        def _():
            pass_on(None, low_whole, dp, False, 1).start()

    sib_own = [
        remote(low_quarter, quarter_out.at[dp], sib_own_sem, (0,), sibling),
        remote(low_whole, whole_out.at[dp], sib_own_sem, (1,), sibling),
    ]
    for copy in sib_own:
        copy.start()
    def sources(act):
        def at_distance(distance):
            @pl.when(z >= distance)
            def _():
                act(dp - 2 * distance, True, z < nz - 1)

            @pl.when(z + distance < nz)
            def _():
                act(dp + 2 * distance, False, z > 0)

        return at_distance

    def forward(ref_view, at, slot):
        return remote(ref_view, ref_view, sib_sem, (slot, at // 2), sibling)

    def one_x(at):
        view = quarter_out.at[at, y, x, 0]
        return remote(view, view, one_sem, (0, at // 2), x_peer)

    def one_y(at):
        view = quarter_out.at[at, y, x, 1]
        return remote(view, view, one_sem, (1, at // 2), y_peer)

    def two_y(at):
        view = quarter_out.at[at, y, :, 0]
        return remote(view, view, two_sem, (0, at // 2), y_peer)

    def two_x(at):
        view = quarter_out.at[at, :, x, 1]
        return remote(view, view, two_sem, (1, at // 2), x_peer)

    def sib_views(at):
        return [
            quarter_out.at[at, y, x],
            quarter_out.at[at, y, 1 - x, 0],
            quarter_out.at[at, 1 - y, x, 1],
            quarter_out.at[at, 1 - y, :, 0],
            quarter_out.at[at, :, 1 - x, 1],
            whole_out.at[at],
        ]

    def quarter_came(at, upward, onward):
        view = quarter_out.at[at, y, x]
        pass_on(view, None, at, upward, 0).wait_recv()

        @pl.when(onward)
        def _():
            pass_on(view, None, at, upward, 0).start()

        one_x(at).start()
        one_y(at).start()
        forward(sib_views(at)[0], at, 0).start()

    def whole_came(at, upward, onward):
        view = whole_out.at[at]
        pass_on(None, view, at, upward, 1).wait_recv()

        @pl.when(onward)
        def _():
            pass_on(None, view, at, upward, 1).start()

        forward(sib_views(at)[5], at, 5).start()

    def one_came(at, upward, onward):
        one_x(at).wait_recv()
        two_y(at).start()
        forward(sib_views(at)[1], at, 1).start()
        one_y(at).wait_recv()
        two_x(at).start()
        forward(sib_views(at)[2], at, 2).start()

    def two_came(at, upward, onward):
        two_y(at).wait_recv()
        forward(sib_views(at)[3], at, 3).start()
        two_x(at).wait_recv()
        forward(sib_views(at)[4], at, 4).start()

    def finished(at, upward, onward):
        view = quarter_out.at[at, y, x]

        @pl.when(onward)
        def _():
            pass_on(view, None, at, upward, 0).wait_send()
            pass_on(None, whole_out.at[at], at, upward, 1).wait_send()

        one_x(at).wait_send()
        one_y(at).wait_send()
        two_x(at).wait_send()
        two_y(at).wait_send()
        for slot, ref_view in enumerate(sib_views(at)):
            copy = forward(ref_view, at, slot)
            copy.wait_send()
            copy.wait_recv()

    for distance in range(1, nz):
        sources(quarter_came)(distance)
        if distance == nz - 1:
            sources(one_came)(1)
        own_whole(distance)
    plan = [(whole_came, 1)] + [(one_came, d) for d in range(2, nz)]
    for distance in range(2, nz):
        plan += [(whole_came, distance), (two_came, distance - 1)]
    plan += [(two_came, nz - 1)]
    for act, distance in plan:
        sources(act)(distance)
    for distance in range(1, nz):
        sources(finished)(distance)

    @pl.when(above)
    def _():
        pass_on(low_quarter.at[y, x], None, dp, True, 0).wait_send()
        pass_on(None, low_whole, dp, True, 1).wait_send()

    @pl.when(below)
    def _():
        pass_on(low_quarter.at[y, x], None, dp, False, 0).wait_send()
        pass_on(None, low_whole, dp, False, 1).wait_send()

    for copy in swaps[3:]:
        copy.start()
    for copy in own_copies[:1] + swaps[:3] + sib_own:
        copy.wait()
    stores = [pltpu.make_async_copy(tokens_land, tokens_out, out_sem.at[2 * nz])]
    stores[0].start()

    def put(block):
        place = 0
        for index in range(2 * nz):
            place = jnp.where(owners_ref[index] == block, index, place)
        rows = wide.shape[0]
        base = block * rows
        ordered[base : base + full] = whole_out[place]
        for part in range(8):
            start = base + full + part * quarter
            ordered[start : start + quarter] = quarter_out[
                place, part // 4, part // 2 % 2, part % 2
            ]
        table = pl.ds(base, rows)
        return pltpu.make_async_copy(ordered.at[table], table_out.at[table], out_sem.at[block])

    early = -(-4 * D // wide.shape[0])
    for block in range(early):
        stores.append(put(block))
        stores[-1].start()

    results = []

    def give(src, dst):
        copy = pltpu.make_async_copy(src, dst, work_sem.at[len(results)])
        results.append(copy)
        return copy

    for p in range(passages):
        project(
            tokens_land[p], ordered, vec_ref, q_all.at[p], k_all.at[p], v_all.at[p], v_turned.at[p]
        )
    for src, dst in ((q_all, q_out), (k_all, k_out), (v_all, v_out)):
        give(src, dst).start()
    pairs = HEADS // 2
    lengths = [lengths_ref[blk * passages + p] for p in range(passages)]

    def finish(p):
        first_norm(
            tokens_land[p], ctx_all[p], ordered, vec_ref, normed_all.at[p], inv_all.at[p]
        )
        for src, dst in (
            (ctx_all, ctx_out),
            (normed_all, normed_out),
            (inv_all, inv_out),
            (lse_all, lse_out),
        ):
            give(src.at[p], dst.at[p]).start()

    for p in range(passages):

        @pl.loop(0, pairs)
        def _(pair, p=p):
            for slot in range(pairs):
                block = early + p * pairs + slot
                if block < 2 * nz:

                    @pl.when(pair == slot)
                    def _(block=block):
                        put(block).start()

            attend_pair(
                pair,
                lengths[p],
                q_all.at[p],
                k_all.at[p],
                v_turned.at[p],
                lse_all.at[p],
                ctx_all.at[p],
                ctx_turned,
                scores,
                weights,
            )

        if p == passages - 1:
            for copy in own_copies[1:] + swaps[3:]:
                copy.wait()
            give(cot_land, cot_out).start()
        finish(p)
    for block in range(early, 2 * nz):
        table = pl.ds(block * wide.shape[0], wide.shape[0])
        stores.append(
            pltpu.make_async_copy(ordered.at[table], table_out.at[table], out_sem.at[block])
        )
    for copy in stores + results:
        copy.wait()


def enter(nz, full, owners, tokens, cotangent, master, lengths, vectors):
    f32, low = jnp.float32, jnp.bfloat16
    rows = master.shape[0]
    quarter = (rows - full) // 8
    shares, span, _ = tokens.shape
    passages, span = shares // 4, 4 * span
    swapped = (passages, span, D)
    any_spec = pl.BlockSpec(memory_space=pl.ANY)
    smem = pl.BlockSpec(memory_space=pltpu.SMEM)
    dma = pltpu.SemaphoreType.DMA
    shape = lambda kind: jax.ShapeDtypeStruct(swapped, kind)
    lse = (passages, HEADS, 1, span)
    return pl.pallas_call(
        functools.partial(enter_kernel, nz, full),
        out_shape=(
            shape(low),
            shape(low),
            jax.ShapeDtypeStruct((2 * nz * rows, D), low),
            shape(low),
            shape(low),
            shape(low),
            jax.ShapeDtypeStruct(lse, f32),
            shape(low),
            shape(f32),
            jax.ShapeDtypeStruct((passages, span, 128), f32),
            jax.ShapeDtypeStruct((VEC_LEN // D, D), f32),
        ),
        in_specs=[smem] + [any_spec] * 3 + [smem, pl.BlockSpec(memory_space=pltpu.VMEM)],
        out_specs=[any_spec] * 10 + [pl.BlockSpec(memory_space=pltpu.VMEM)],
        scratch_shapes=[
            pltpu.VMEM((rows, D), f32),
            pltpu.VMEM((2 * quarter, D), f32),
            pltpu.VMEM(swapped, low),
            pltpu.VMEM(swapped, low),
            pltpu.VMEM((2 * nz, full, D), low),
            pltpu.VMEM((2 * nz, 2, 2, 2, quarter, D), low),
            pltpu.VMEM((2 * nz * rows, D), low),
            dma((2,)),
            dma((2, 2, 3)),
            dma((2,)),
            dma((2, 2, 2, nz)),
            dma((2, 2, nz)),
            dma((2, 2, nz)),
            dma((2, 6, nz)),
            dma((2, 2)),
            dma((2 * nz + 1,)),
            pltpu.VMEM(swapped, low),
            pltpu.VMEM(swapped, low),
            pltpu.VMEM(swapped, low),
            pltpu.VMEM((passages, D, span), low),
            pltpu.VMEM(lse, f32),
            pltpu.VMEM(swapped, low),
            pltpu.VMEM(swapped, f32),
            pltpu.VMEM((passages, span, 128), f32),
            pltpu.VMEM((128, span), f32),
            pltpu.VMEM((2, span, span // 2), f32),
            pltpu.VMEM((2, span, span // 2), low),
            dma((4 + 4 * passages,)),
        ],
        compiler_params=pltpu.CompilerParams(
            collective_id=2, has_side_effects=True, vmem_limit_bytes=60 * 1024 * 1024
        ),
        cost_estimate=pl.CostEstimate(
            flops=passages * span * (8 * D * D + 4 * D * span),
            bytes_accessed=6 * 10**7,
            transcendentals=passages * HEADS * span * span,
        ),
        name="enter",
    )(owners, tokens, cotangent, master, lengths, vectors.reshape(-1, 128))


def tail_kernel(
    nz,
    owners_ref,
    qkv_ref,
    back_ref,
    vec_ref,
    d_tokens_ref,
    own_ref,
    vec_sum_ref,
    norm_ref,
    d_tokens_out,
    acc,
    core_land,
    land_one,
    land_two,
    load_sem,
    core_sem,
    one_sem,
    two_sem,
    part,
    mine,
    up_land,
    down_land,
    up_send,
    down_send,
    own_part,
    assembled,
    vec_send,
    vec_land,
    sq_send,
    sq_land,
    part_sem,
    up_sem,
    down_sem,
    gather_sem,
    vec_sem,
    sq_sem,
    out_sem,
    *swap_refs,
):
    dp, blk, z, c, y, x, sibling, x_peer, y_peer = place_of()

    def z_peer(hop):
        return (blk, 2 * lax.rem(z + hop, nz) + c)

    def send(src, dst, sems, slot, device):
        copy = remote_copy(src, dst, sems, slot, device)
        copy.start()
        return copy

    swaps = [
        PositionSwap(d_tokens_ref, d_tokens_out, *swap_refs),
    ]
    partners = [sibling, x_peer, y_peer, swaps[0].diagonal] + [z_peer(h) for h in range(1, nz)]
    barrier = greet(partners)
    late = qkv_ref.shape[0]
    load = pltpu.make_async_copy(back_ref, part.at[pl.ds(late, back_ref.shape[0])], part_sem)
    load.start()
    sems = (load_sem, core_sem, one_sem, two_sem)
    summed = PlaneSum((qkv_ref,), QKV_COUNTS, acc, core_land, land_one, land_two, part, sems)
    slots = range(len(summed.chunks))
    for row in range(VEC_LEN // D):
        for col in range(D // 128):
            at = row * (D // 128) + col
            vec_send[0, at : at + 1] = vec_ref[row : row + 1, col * 128 : (col + 1) * 128]
    pl.semaphore_wait(barrier, len(partners))
    summed.begin(slots)

    def vec_copy(turn):
        peer = (sibling, x_peer, y_peer)[turn]
        return remote_copy(vec_send.at[turn], vec_land.at[turn], vec_sem, turn, peer)

    def vec_next(turn):
        vec_copy(turn).wait()
        vec_send[turn + 1] = vec_send[turn] + vec_land[turn]
        if turn < 2:
            vec_copy(turn + 1).start()

    vec_copy(0).start()
    summed.paired(slots)
    vec_next(0)
    vec_next(1)
    vec_next(2)
    vec_z = [
        send(vec_send.at[3], vec_land.at[3 + z], vec_sem, 2 + hop, z_peer(hop))
        for hop in range(1, nz)
    ]
    summed.crossed(slots)
    load.wait()
    summed.settled(slots)
    for swap in swaps:
        swap.begin()

    grains = part.shape[0] // (2 * nz)
    for block in range(2 * nz):
        place = owners_ref[block] * grains
        for g in range(grains):
            mine[block, g] = part[place + g]

    def gather(turn, piece):
        views = (
            (own_part.at[1 - c, piece], assembled.at[piece, c, y, x], sibling),
            (assembled.at[piece, 0, y, x], assembled.at[piece, 0, y, x], x_peer),
            (assembled.at[piece, 1, y, x], assembled.at[piece, 1, y, x], y_peer),
            (assembled.at[piece, 0, y], assembled.at[piece, 0, y], y_peer),
            (assembled.at[piece, 1, :, x], assembled.at[piece, 1, :, x], x_peer),
        )
        src, dst, peer = views[turn]
        return remote_copy(src, dst, gather_sem, turn * grains + piece, peer)

    def chain(zv):
        unit, wait = 3.0, 2.5
        steps, copies = [], []

        def message(upward, d, piece):
            land, sends, sems = (
                (up_land, up_send, up_sem) if upward else (down_land, down_send, down_sem)
            )
            target = (blk, dp + 2 if upward else dp - 2)
            return remote_copy(
                sends.at[d, piece], land.at[d, piece], sems, d * grains + piece, target
            )

        def passing(upward, d, piece):
            def run():
                land, sends = (up_land, up_send) if upward else (down_land, down_send)
                fed = zv > 0 if upward else zv < nz - 1
                copy = message(upward, d, piece)
                if fed:
                    copy.wait_recv()
                for j in range(2):
                    value = mine[2 * d + j, piece]
                    if fed:
                        value = add_low(value, land[d, piece, j])
                    sends[d, piece, j] = value
                copy.start()
                copies.append(copy)

            return run

        def arrived(piece):
            if zv > 0:
                message(True, zv, piece).wait_recv()
            if zv < nz - 1:
                message(False, zv, piece).wait_recv()
            squares = jnp.zeros((8, D), jnp.float32)
            for j in range(2):
                value = mine[2 * zv + j, piece].astype(jnp.float32)
                if zv > 0:
                    value = value + up_land[zv, piece, j].astype(jnp.float32)
                if zv < nz - 1:
                    value = value + down_land[zv, piece, j].astype(jnp.float32)
                rounded = value.astype(jnp.bfloat16)
                own_part[j, piece] = rounded
                again = rounded.astype(jnp.float32)
                squares = squares + jnp.sum((again * again).reshape(-1, 8, D), axis=0)
            total = squares[:, 0:128]
            for col in range(1, D // 128):
                total = total + squares[:, col * 128 : (col + 1) * 128]
            sq_send[0] = total if piece == 0 else sq_send[0] + total
            assembled[piece, c, y, x] = own_part[c, piece]
            gather(0, piece).start()

        def over_pair(piece):
            gather(0, piece).wait()
            gather(1, piece).start()
            gather(2, piece).start()

        def over_plane(piece):
            gather(1, piece).wait()
            gather(3, piece).start()
            gather(2, piece).wait()
            gather(4, piece).start()

        for piece in range(grains):
            first = piece * (nz - 1)
            for d in range(zv + 1, nz):
                at = (zv + first + nz - 1 - d) * unit + zv * wait
                steps.append((at, passing(True, d, piece)))
            for d in range(zv):
                at = (nz - 1 - zv + first + d) * unit + (nz - 1 - zv) * wait
                steps.append((at, passing(False, d, piece)))
            end = (first + nz - 1) * unit + (nz - 1) * wait
            steps.append((end, functools.partial(arrived, piece)))
            if piece < grains - 1:
                steps.append((end + 5.0, functools.partial(over_pair, piece)))
                steps.append((end + 9.5, functools.partial(over_plane, piece)))
        for _, step in sorted(steps, key=lambda entry: entry[0]):
            step()
        for copy in copies:
            copy.wait_send()
        sq = remote_copy(sq_send.at[0], sq_land.at[0], sq_sem, 0, sibling)
        sq.start()
        over_pair(grains - 1)
        sq.wait()

    for zv in range(nz):
        run_when(z == zv, functools.partial(chain, zv))

    for swap in swaps:
        swap.passed()
    sq_send[1] = sq_send[0] + sq_land[0]
    sq = send(sq_send.at[1], sq_land.at[1], sq_sem, 1, x_peer)
    sq.wait()
    sq_send[2] = sq_send[1] + sq_land[1]
    sq = send(sq_send.at[2], sq_land.at[2], sq_sem, 2, y_peer)
    last = grains - 1
    gather(1, last).wait()
    gather(3, last).start()
    gather(2, last).wait()
    gather(4, last).start()
    sq.wait()
    sq_send[3] = sq_send[2] + sq_land[2]
    sq_z = [
        send(sq_send.at[3], sq_land.at[3 + z], sq_sem, 2 + hop, z_peer(hop)) for hop in range(1, nz)
    ]
    for copy in vec_z + sq_z:
        copy.wait()
    vec_land[3 + z] = vec_send[3]
    sq_land[3 + z] = sq_send[3]
    vec_total, sq_total = vec_land[3], sq_land[3]
    for other in range(1, nz):
        vec_total = vec_total + vec_land[3 + other]
        sq_total = sq_total + sq_land[3 + other]
    vec_sum_ref[...] = vec_total
    grad_norm = jnp.sqrt(
        jnp.sum(sq_total, keepdims=True) + jnp.sum(vec_total * vec_total, keepdims=True)
    )
    norm_ref[...] = grad_norm
    done = []
    for piece in range(grains):
        gather(3, piece).wait()
        gather(4, piece).wait()
        done.append(pltpu.make_async_copy(assembled.at[piece], own_ref.at[piece], out_sem.at[piece]))
        done[-1].start()
    for swap in swaps:
        swap.end()
    for copy in done:
        copy.wait()


def tail(nz, owners, g_qkv, back, grad_vector, d_tokens):
    low, f32 = jnp.bfloat16, jnp.float32
    passages, span, _ = d_tokens.shape
    swapped = jax.ShapeDtypeStruct((4 * passages, span // 4, D), low)
    granules = g_qkv.shape[0] + back.shape[0]
    grains = granules // (2 * nz)
    any_spec = pl.BlockSpec(memory_space=pl.ANY)
    vmem = pl.BlockSpec(memory_space=pltpu.VMEM)
    dma = pltpu.SemaphoreType.DMA
    block = lambda *lead: pltpu.VMEM((*lead, GRAIN, D), low)
    lanes = (VEC_LEN // 128, 128)
    return pl.pallas_call(
        functools.partial(tail_kernel, nz),
        out_shape=(
            jax.ShapeDtypeStruct((grains, 2, 2, 2, GRAIN, D), low),
            jax.ShapeDtypeStruct(lanes, f32),
            jax.ShapeDtypeStruct((1, 1), f32),
            swapped,
        ),
        in_specs=[pl.BlockSpec(memory_space=pltpu.SMEM)]
        + [any_spec] * 2
        + [vmem, any_spec],
        out_specs=(any_spec, vmem, vmem, any_spec),
        scratch_shapes=PlaneSum.scratch(QKV_COUNTS, with_part=False)
        + [
            block(granules),
            block(2 * nz, grains),
            block(nz, grains, 2),
            block(nz, grains, 2),
            block(nz, grains, 2),
            block(nz, grains, 2),
            block(2, grains),
            block(grains, 2, 2, 2),
            pltpu.VMEM((4, *lanes), f32),
            pltpu.VMEM((3 + nz, *lanes), f32),
            pltpu.VMEM((4, 8, 128), f32),
            pltpu.VMEM((3 + nz, 8, 128), f32),
            dma(()),
            dma((2, nz * grains)),
            dma((2, nz * grains)),
            dma((2, 5 * grains)),
            dma((2, 2 + nz)),
            dma((2, 2 + nz)),
            dma((grains,)),
        ]
        + PositionSwap.scratch(passages, span),
        compiler_params=pltpu.CompilerParams(
            collective_id=1, has_side_effects=True, vmem_limit_bytes=60 * 1024 * 1024
        ),
        cost_estimate=pl.CostEstimate(flops=10**7, bytes_accessed=3 * 10**7, transcendentals=0),
        name="grad_tail",
    )(owners, g_qkv, back, grad_vector, d_tokens)


def keep_lanes(rows, half):
    lane = lax.broadcasted_iota(jnp.int32, rows.shape, 1)
    keep = lane < HEAD_DIM if half == 0 else lane >= HEAD_DIM
    return jnp.where(keep, rows, jnp.zeros_like(rows))


def norm_rows(mixed):
    row_mean = jnp.mean(mixed, axis=-1, keepdims=True)
    centred = mixed - row_mean
    inv_std = lax.rsqrt(jnp.mean(centred * centred, axis=-1, keepdims=True) + 1e-12)
    return centred * inv_std, inv_std


def project(x, w_ref, vec_ref, q_out, k_out, v_out, v_turned):
    f32, low = jnp.float32, jnp.bfloat16

    def product(lo):
        return jnp.dot(x, w_ref[lo : lo + D], preferred_element_type=f32)

    q_out[...] = ((product(0) + vec_ref[0:1]).astype(low).astype(f32) * 0.125).astype(low)
    k_out[...] = product(D).astype(low)
    values = product(2 * D) + vec_ref[1:2]
    v_out[...] = values.astype(low)
    v_turned[...] = values.T.astype(low)


def attend_pair(pair, length, q_ref, k_ref, v_turned, lse_ref, ctx_ref, ctx_turned, scores, weights):
    f32, low = jnp.float32, jnp.bfloat16
    span = q_ref.shape[0]
    width, strip = span // 2, 64
    lanes = pl.ds(pl.multiple_of(pair * 128, 128), 128)
    keys = k_ref[:, lanes]
    head_keys = [keep_lanes(keys, half) for half in range(2)]
    units = [(half, part) for half in range(2) for part in range(2)]

    def score(unit):
        half, part = units[unit]
        scores[unit % 2] = contract_cols(head_keys[half], q_ref[part * width : (part + 1) * width, lanes])

    def masked(unit, at):
        row = at + lax.broadcasted_iota(jnp.int32, (strip, width), 0)
        return jnp.where(row < length, scores[unit % 2, at : at + strip], -1000000000.0)

    def fold(value, op):
        return op(value.reshape(strip // 8, 8, width), axis=0)

    score(0)
    for unit, (half, part) in enumerate(units):
        if unit + 1 < len(units):
            score(unit + 1)
        cols = pl.ds(part * width, width)
        tops = fold(masked(unit, 0), jnp.max)
        for at in range(strip, span, strip):
            tops = jnp.maximum(tops, fold(masked(unit, at), jnp.max))
        peak = jnp.max(tops, axis=0, keepdims=True)
        sums = jnp.zeros((8, width), f32)
        for at in range(0, span, strip):
            weight = jnp.exp(masked(unit, at) - peak)
            sums = sums + fold(weight, jnp.sum)
            weights[unit % 2, at : at + strip] = weight.astype(low)
        total = jnp.sum(sums, axis=0, keepdims=True)
        lse_ref[2 * pair + half, :, cols] = peak + jnp.log(total)
        turned = v_turned[pl.ds(pl.multiple_of(pair * 128 + half * 64, 64), 64), :]
        out = jnp.dot(turned, weights[unit % 2], preferred_element_type=f32)
        ctx_turned[half * 64 : half * 64 + 64, cols] = out / total
    ctx_ref[:, lanes] = ctx_turned[...].T.astype(low)


def first_norm(x, ctx, w_ref, vec_ref, normed_ref, inv_ref):
    attn_out = jnp.dot(ctx, w_ref[3 * D : 4 * D], preferred_element_type=jnp.float32)
    normed, inv_std = norm_rows(x.astype(jnp.float32) + (attn_out + vec_ref[2:3]))
    normed_ref[...] = normed
    inv_ref[...] = jnp.broadcast_to(inv_std, inv_ref.shape)


def attend_kernel(
    lengths_ref,
    x_ref,
    w_ref,
    vec_ref,
    q_ref,
    k_ref,
    v_ref,
    lse_ref,
    ctx_ref,
    normed_ref,
    inv_ref,
    v_turned,
    ctx_turned,
    scores,
    weights,
):
    length = lengths_ref[lax.axis_index("blk") * pl.num_programs(0) + pl.program_id(0)]
    x = x_ref[0]
    project(x, w_ref, vec_ref, q_ref.at[0], k_ref.at[0], v_ref.at[0], v_turned)

    @pl.loop(0, HEADS // 2)
    def _(pair):
        attend_pair(
            pair,
            length,
            q_ref.at[0],
            k_ref.at[0],
            v_turned,
            lse_ref.at[0],
            ctx_ref.at[0],
            ctx_turned,
            scores,
            weights,
        )

    first_norm(x, ctx_ref[0], w_ref, vec_ref, normed_ref.at[0], inv_ref.at[0])


def attend(lengths, tokens, table, vec_rows):
    f32, low = jnp.float32, jnp.bfloat16
    passages, span, _ = tokens.shape
    rows = pl.BlockSpec((1, span, D), lambda p: (p, 0, 0))
    shape = lambda kind: jax.ShapeDtypeStruct((passages, span, D), kind)
    return pl.pallas_call(
        attend_kernel,
        grid=(passages,),
        out_shape=(
            shape(low),
            shape(low),
            shape(low),
            jax.ShapeDtypeStruct((passages, HEADS, 1, span), f32),
            shape(low),
            shape(f32),
            jax.ShapeDtypeStruct((passages, span, 128), f32),
        ),
        in_specs=[
            pl.BlockSpec(memory_space=pltpu.SMEM),
            rows,
            pl.BlockSpec((4 * D, D), lambda p: (0, 0)),
            pl.BlockSpec((VEC_LEN // D, D), lambda p: (0, 0)),
        ],
        out_specs=(
            rows,
            rows,
            rows,
            pl.BlockSpec((1, HEADS, 1, span), lambda p: (p, 0, 0, 0)),
            rows,
            rows,
            pl.BlockSpec((1, span, 128), lambda p: (p, 0, 0)),
        ),
        scratch_shapes=[
            pltpu.VMEM((D, span), low),
            pltpu.VMEM((128, span), f32),
            pltpu.VMEM((2, span, span // 2), f32),
            pltpu.VMEM((2, span, span // 2), low),
        ],
        compiler_params=pltpu.CompilerParams(vmem_limit_bytes=56 * 1024 * 1024),
        cost_estimate=pl.CostEstimate(
            flops=passages * span * (8 * D * D + 4 * D * span),
            bytes_accessed=passages * span * D * 20,
            transcendentals=passages * HEADS * span * span,
        ),
        name="attend",
    )(lengths, tokens, table, vec_rows)


def plane_chunks(counts):
    chunks, base = [], 0
    for source, count in enumerate(counts):
        half = count // 2
        step = half if half % 2 else 2
        for first in range(0, half, step):
            chunks.append((source, first, step, base + first, True))
            chunks.append((source, half + first, step, base + half + first, False))
        base += count
    return chunks


def plane_order(granules):
    half = granules // 2

    def order(turn):
        pair = turn // 2
        return lax.rem(pair, 2) * half + (pair // 2) * 2 + lax.rem(turn, 2)

    return order


def place_of():
    dp, blk = lax.axis_index("dp"), lax.axis_index("blk")
    z, c, y, x = dp // 2, dp % 2, blk // 2, blk % 2
    sibling = (blk, 2 * z + 1 - c)
    x_peer = (2 * y + 1 - x, dp)
    y_peer = (2 * (1 - y) + x, dp)
    return dp, blk, z, c, y, x, sibling, x_peer, y_peer


def remote_copy(src, dst, sems, slot, device):
    return pltpu.make_async_remote_copy(
        src_ref=src,
        dst_ref=dst,
        send_sem=sems.at[0, slot],
        recv_sem=sems.at[1, slot],
        device_id=device,
        device_id_type=MESH,
    )


class PlaneSum:
    def __init__(self, sources, counts, acc, core_land, one_land, two_land, part, sems, base=0):
        self.sources, self.acc, self.core_land = sources, acc, core_land
        self.one_land, self.two_land, self.part, self.base = one_land, two_land, part, base
        self.load_sem, self.core_sem, self.one_sem, self.two_sem = sems
        self.chunks = plane_chunks(counts)
        self.place = place_of()

    def load(self, slot):
        source, first, count, at, _ = self.chunks[slot]
        return pltpu.make_async_copy(
            self.sources[source].at[pl.ds(first, count), self.place[3]],
            self.acc.at[pl.ds(at, count)],
            self.load_sem.at[slot],
        )

    def core(self, slot):
        source, first, count, at, _ = self.chunks[slot]
        return remote_copy(
            self.sources[source].at[pl.ds(first, count), 1 - self.place[3]],
            self.core_land.at[pl.ds(at, count)],
            self.core_sem,
            slot,
            self.place[6],
        )

    def one(self, slot):
        _, _, count, at, x_first = self.chunks[slot]
        _, _, _, _, y, x, _, x_peer, y_peer = self.place
        rows = pl.ds(at, count)
        view = self.acc.at[rows, :, 1 - x] if x_first else self.acc.at[rows, 1 - y]
        return remote_copy(
            view, self.one_land.at[rows], self.one_sem, slot, x_peer if x_first else y_peer
        )

    def two(self, slot):
        _, _, count, at, x_first = self.chunks[slot]
        _, _, _, _, y, x, _, x_peer, y_peer = self.place
        rows = pl.ds(at, count)
        view = self.acc.at[rows, 1 - y, x] if x_first else self.acc.at[rows, y, 1 - x]
        return remote_copy(
            view, self.two_land.at[rows], self.two_sem, slot, y_peer if x_first else x_peer
        )

    def begin(self, slots):
        for slot in slots:
            self.load(slot).start()
            self.core(slot).start()

    def paired(self, slots):
        for slot in slots:
            self.load(slot).wait()
            self.core(slot).wait()
            _, _, count, at, _ = self.chunks[slot]

            @pl.loop(at, at + count)
            def _(g):
                self.acc[g] = add_low(self.acc[g], self.core_land[g])

            self.one(slot).start()

    def crossed(self, slots):
        _, _, _, _, y, x, _, _, _ = self.place
        for slot in slots:
            self.one(slot).wait()
            _, _, count, at, x_first = self.chunks[slot]

            @pl.loop(at, at + count)
            def _(g):
                for side in range(2):
                    if x_first:
                        self.acc[g, side, x] = add_low(self.acc[g, side, x], self.one_land[g, side])
                    else:
                        self.acc[g, y, side] = add_low(self.acc[g, y, side], self.one_land[g, side])

            self.two(slot).start()

    def half_settled(self, slots, red_ref, red_sem):
        _, _, _, _, y, x, _, _, _ = self.place
        for slot in slots:
            self.one(slot).wait()
            _, _, count, at, x_first = self.chunks[slot]

            @pl.loop(at, at + count)
            def _(g):
                for side in range(2):
                    if x_first:
                        self.acc[g, side, x] = add_low(self.acc[g, side, x], self.one_land[g, side])
                    else:
                        self.acc[g, y, side] = add_low(self.acc[g, y, side], self.one_land[g, side])

            self.kept(slot, red_ref, red_sem).start()

    def kept(self, slot, red_ref, red_sem):
        _, _, count, at, x_first = self.chunks[slot]
        _, _, _, _, y, x, _, _, _ = self.place
        rows = pl.ds(at, count)
        view = self.acc.at[rows, :, x] if x_first else self.acc.at[rows, y]
        return pltpu.make_async_copy(view, red_ref.at[rows], red_sem.at[slot])

    def settled(self, slots):
        _, _, _, _, y, x, _, _, _ = self.place
        for slot in slots:
            self.two(slot).wait()
            _, _, count, at, _ = self.chunks[slot]

            @pl.loop(at, at + count)
            def _(g):
                self.part[self.base + g] = add_low(self.acc[g, y, x], self.two_land[g])

    @staticmethod
    def scratch(counts, with_part=True):
        low, dma = jnp.bfloat16, pltpu.SemaphoreType.DMA
        total, slots = sum(counts), len(plane_chunks(counts))
        shapes = [
            pltpu.VMEM((total, 2, 2, GRAIN, D), low),
            pltpu.VMEM((total, 2, 2, GRAIN, D), low),
            pltpu.VMEM((total, 2, GRAIN, D), low),
            pltpu.VMEM((total, GRAIN, D), low),
            dma((slots,)),
            dma((2, slots)),
            dma((2, slots)),
            dma((2, slots)),
        ]
        return shapes + ([pltpu.VMEM((total, GRAIN, D), low)] if with_part else [])


class SecondStep:
    def __init__(self, red_ref, counts, keep, land, part, load_sem, two_sem, base):
        _, _, _, _, y, x, _, x_peer, y_peer = place_of()
        self.keep, self.land, self.part, self.base = keep, land, part, base
        self.chunks = plane_chunks(counts)
        self.loads, self.sends = [], []
        for slot, (_, _, count, at, x_first) in enumerate(self.chunks):
            rows = pl.ds(at, count)
            near, far, peer = (y, 1 - y, y_peer) if x_first else (x, 1 - x, x_peer)
            self.loads.append(
                pltpu.make_async_copy(red_ref.at[rows, near], keep.at[rows], load_sem.at[slot])
            )
            self.sends.append(
                remote_copy(red_ref.at[rows, far], land.at[rows], two_sem, slot, peer)
            )

    def begin(self):
        for copy in self.loads + self.sends:
            copy.start()

    def end(self):
        for slot, (_, _, count, at, _) in enumerate(self.chunks):
            self.loads[slot].wait()
            self.sends[slot].wait()

            @pl.loop(at, at + count)
            def _(g):
                self.part[self.base + g] = add_low(self.keep[g], self.land[g])

    @staticmethod
    def scratch(counts):
        low, dma = jnp.bfloat16, pltpu.SemaphoreType.DMA
        total, slots = sum(counts), len(plane_chunks(counts))
        block = pltpu.VMEM((total, GRAIN, D), low)
        return [block, block, dma((slots,)), dma((2, slots))]


def run_when(condition, task):
    @pl.when(condition)
    def _():
        task()


def greet(partners):
    barrier = pltpu.get_barrier_semaphore()
    for partner in partners:
        pl.semaphore_signal(barrier, inc=1, device_id=partner, device_id_type=MESH)
    return barrier


class PositionSwap:
    def __init__(self, rows_in, rows_out, keep, keep_sem, swap_sem):
        dp, blk, _, _, _, _, _, x_peer, y_peer = place_of()
        passages, span = rows_in.shape[0], rows_out.shape[1]
        self.diagonal = (3 - blk, dp)
        at = pl.ds(blk * passages, passages)
        self.first = pltpu.make_async_copy(
            rows_in.at[:, pl.ds(blk * span, span)], keep, keep_sem.at[0]
        )
        self.second = pltpu.make_async_copy(keep, rows_out.at[at], keep_sem.at[1])
        self.pushes = [
            remote_copy(
                rows_in.at[:, pl.ds(peer[0] * span, span)], rows_out.at[at], swap_sem, slot, peer
            )
            for slot, peer in enumerate((x_peer, y_peer, self.diagonal))
        ]

    def begin(self):
        for copy in [self.first] + self.pushes:
            copy.start()

    def passed(self):
        self.first.wait()
        self.second.start()

    def end(self):
        for copy in [self.second] + self.pushes:
            copy.wait()

    @staticmethod
    def scratch(passages, span):
        dma = pltpu.SemaphoreType.DMA
        return [pltpu.VMEM((passages, span // 4, D), jnp.bfloat16), dma((2,)), dma((2, 3))]


def attend_back_kernel(
    lengths_ref,
    x_ref,
    w_ref,
    q_ref,
    k_ref,
    v_ref,
    lse_ref,
    d_ctx_ref,
    d_mixed_ref,
    vec_in_ref,
    *refs,
):
    f32, low = jnp.float32, jnp.bfloat16
    beside = len(refs) > 9
    tasks = {}
    if beside:
        *sources, outer_red, refs = *refs[:3], refs[3:]
        red_ref, refs = refs[3], refs[:3] + refs[4:]
        extra, refs = refs[9:], refs[:9]
        acc, core_land, one_land, two_land, *sems, keep, land, keep_sem, keep_two, share, red_sem = extra
    grad_ref, table_ref, vec_ref, k_turned, dq_turned, dq_all, dk_all, dv_all, x_all = refs
    passage = pl.program_id(0)
    if beside:
        summed = PlaneSum(sources, BACK_COUNTS, acc, core_land, one_land, two_land, share, sems)
        second = SecondStep(
            outer_red, OUTER_COUNTS, keep, land, share, keep_sem, keep_two, sum(BACK_COUNTS)
        )
        slots = range(len(summed.chunks))

        @pl.when(passage == 0)
        def _():
            greet(summed.place[6:])

        def begin():
            pl.semaphore_wait(pltpu.get_barrier_semaphore(), 3)
            summed.begin(slots)
            second.begin()

        tasks = {
            0: begin,
            3: lambda: summed.paired(slots),
            5: second.end,
            9: lambda: summed.crossed(slots),
        }

        def end():
            summed.settled(slots)
            stored = pltpu.make_async_copy(share, red_ref, red_sem)
            stored.start()
            stored.wait()

    span = x_ref.shape[1]
    half_span = span // 2
    length = lengths_ref[lax.axis_index("blk") * pl.num_programs(0) + passage]
    rows = pl.ds(pl.multiple_of(passage * span, span), span)
    x_all[rows, :] = x_ref[0]
    k_turned[...] = k_ref[0].astype(f32).T.astype(low)
    valid = lax.broadcasted_iota(jnp.int32, (span, half_span), 0) < length

    @pl.loop(0, HEADS // 2)
    def _(pair):
        slot = passage * (HEADS // 2) + pair
        for at in sorted(tasks):
            run_when(slot == at, tasks[at])
        lanes = pl.ds(pl.multiple_of(pair * 128, 128), 128)
        keys, values = k_ref[0, :, lanes], v_ref[0, :, lanes]
        dk, dv = jnp.zeros((span, 128), f32), jnp.zeros((span, 128), f32)
        for half in range(2):
            head_keys, head_values = keep_lanes(keys, half), keep_lanes(values, half)
            turned = k_turned[pl.ds(pl.multiple_of(pair * 128 + half * 64, 64), 64), :]
            for part in range(2):
                cols = pl.ds(part * half_span, half_span)
                queries = q_ref[0, cols, lanes]
                d_out = d_ctx_ref[0, cols, lanes]
                scores = contract_cols(head_keys, queries)
                scores = jnp.where(valid, scores, -1000000000.0)
                probs = jnp.exp(scores - lse_ref[0, 2 * pair + half, :, cols])
                dv = dv + jnp.dot(
                    probs.astype(low), keep_lanes(d_out, half), preferred_element_type=f32
                )
                d_probs = contract_cols(head_values, d_out)
                weighted = probs * d_probs
                inner = jnp.sum(weighted, axis=0, keepdims=True)
                d_scores = (weighted - probs * inner).astype(low)
                dk = dk + jnp.dot(d_scores, keep_lanes(queries, half), preferred_element_type=f32)
                dq_turned[half * 64 : half * 64 + 64, cols] = (
                    jnp.dot(turned, d_scores, preferred_element_type=f32) * 0.125
                )
        dq_all[rows, lanes] = dq_turned[...].T.astype(low)
        dk_all[rows, lanes] = dk.astype(low)
        dv_all[rows, lanes] = dv.astype(low)

    grad = d_mixed_ref[0]
    for lo, part in ((0, dq_all), (D, dk_all), (2 * D, dv_all)):
        grad = grad + contract_cols(part[rows, :], w_ref[lo : lo + D])
    grad_ref[0] = grad.astype(low)

    @pl.when(passage == pl.num_programs(0) - 1)
    def _():
        for lo, part in ((0, dq_all), (D, dk_all), (2 * D, dv_all)):
            table_ref[lo : lo + D] = contract_rows(x_all[...], part[...]).astype(low)
        if beside:
            end()
        vec_ref[...] = vec_in_ref[...]
        vec_ref[0:1] = jnp.sum(dq_all[...].astype(f32), axis=0, keepdims=True)
        vec_ref[1:2] = jnp.sum(dv_all[...].astype(f32), axis=0, keepdims=True)


def attend_back(
    lengths, tokens, table, queries, keys, values, lse, d_ctx, d_mixed, vec_grad, sources=()
):
    f32, low = jnp.float32, jnp.bfloat16
    passages, span, _ = tokens.shape
    rows = pl.BlockSpec((1, span, D), lambda p: (p, 0, 0))
    whole = pltpu.VMEM((passages * span, D), low)
    any_spec = pl.BlockSpec(memory_space=pl.ANY)
    red_shape, beside, extra, more = (), [], {}, ()
    if sources:
        total = sum(BACK_COUNTS) + sum(OUTER_COUNTS)
        red_shape = (jax.ShapeDtypeStruct((total, GRAIN, D), low),)
        beside = PlaneSum.scratch(BACK_COUNTS, with_part=False) + SecondStep.scratch(OUTER_COUNTS)
        beside += [pltpu.VMEM((total, GRAIN, D), low), pltpu.SemaphoreType.DMA]
        extra = dict(collective_id=3, has_side_effects=True)
        more = sources
    return pl.pallas_call(
        attend_back_kernel,
        grid=(passages,),
        out_shape=(
            jax.ShapeDtypeStruct((passages, span, D), low),
            jax.ShapeDtypeStruct((3 * D, D), low),
            jax.ShapeDtypeStruct((VEC_LEN // D, D), f32),
        )
        + red_shape,
        in_specs=[
            pl.BlockSpec(memory_space=pltpu.SMEM),
            rows,
            pl.BlockSpec((3 * D, D), lambda p: (0, 0)),
            rows,
            rows,
            rows,
            pl.BlockSpec((1, HEADS, 1, span), lambda p: (p, 0, 0, 0)),
            rows,
            rows,
            pl.BlockSpec((VEC_LEN // D, D), lambda p: (0, 0)),
        ]
        + [any_spec] * len(more),
        out_specs=(
            rows,
            pl.BlockSpec((3 * D, D), lambda p: (0, 0)),
            pl.BlockSpec((VEC_LEN // D, D), lambda p: (0, 0)),
        )
        + (any_spec,) * len(red_shape),
        scratch_shapes=[pltpu.VMEM((D, span), low), pltpu.VMEM((128, span), f32)]
        + [whole] * 4
        + beside,
        compiler_params=pltpu.CompilerParams(vmem_limit_bytes=60 * 1024 * 1024, **extra),
        cost_estimate=pl.CostEstimate(
            flops=passages * span * (12 * D * D + 10 * D * span),
            bytes_accessed=passages * span * D * 24,
            transcendentals=passages * HEADS * span * span,
        ),
        name="attend_back",
    )(lengths, tokens, table, queries, keys, values, lse, d_ctx, d_mixed, vec_grad, *more)


ERFC_SLOPE = 0.42
ERFC_TERMS = (
    0.23681282137224371,
    0.23975548803522717,
    0.19369618325685073,
    0.27205881038432234,
    -0.136659548208163,
    0.44720921707821076,
    -0.32398587364624676,
    0.07111276080879629,
)


def gelu_pair(x):
    slope = 1.0 + (ERFC_SLOPE * math.sqrt(0.5)) * jnp.abs(x)
    t = pltpu.reciprocal(slope, approx=True)
    t = t * (2.0 - slope * t)
    bell = jnp.exp2(x * x * (-0.5 / math.log(2.0)))
    series = 0.5 * ERFC_TERMS[-1]
    for term in ERFC_TERMS[-2::-1]:
        series = series * t + 0.5 * term
    low_side = series * t * bell
    cdf = jnp.where(x < 0.0, low_side, 1.0 - low_side)
    return x * cdf, cdf + x * bell * (1.0 / math.sqrt(2.0 * math.pi))


def ffn_kernel(
    lengths_ref,
    vec_ref,
    normed_ref,
    inv_ref,
    cot_ref,
    ctx_ref,
    table_ref,
    output_ref,
    d_mixed_ref,
    d_ctx_ref,
    vec_grad_ref,
    d_out_ref,
    d_inner_ref,
    d_outer_ref,
    *refs,
):
    beside = len(refs) > 20
    if beside:
        red_ref, refs = refs[0], refs[1:]
    (
        w_out,
        w_inner,
        w_outer,
        normed,
        inv_std,
        cot,
        left_pre,
        right_pre,
        slope,
        active,
        hidden,
        output,
        d_branch,
        d_mixed,
        staged,
        staged_outer,
        load_sem,
        store_sem,
        done_sem,
        wide_sem,
        *extra,
    ) = refs
    f32, low = jnp.float32, jnp.bfloat16
    count = normed.shape[0]
    chunk = left_pre.shape[1]
    chunks = FF // chunk
    tile, strip = 256, 32
    tiles = count // tile
    sources = (
        (normed_ref, normed),
        (table_ref.at[pl.ds(4 * D + FF, FF)], w_outer),
        (cot_ref, cot),
        (inv_ref, inv_std),
        (table_ref.at[pl.ds(3 * D, D)], w_out),
        (ctx_ref, hidden),
    )
    loads = [
        pltpu.make_async_copy(src, dst, load_sem.at[slot])
        for slot, (src, dst) in enumerate(sources)
    ]
    loads[0].start()

    def columns(part):
        return pl.ds(pl.multiple_of(part * chunk, chunk), chunk)

    def load_wide(part):
        rows = pl.ds(4 * D + part * chunk, chunk)
        return pltpu.make_async_copy(
            table_ref.at[rows], w_inner.at[columns(part)], wide_sem.at[part]
        )

    for part in range(chunks):
        load_wide(part).start()
    for load in loads[1:5]:
        load.start()

    if beside:
        acc, core_land, one_land, two_land, *sems, red_sem, swap_sem = extra
        summed = PlaneSum((d_outer_ref,), OUTER_COUNTS, acc, core_land, one_land, None, None, sems)
        dp, blk = summed.place[:2]
        diagonal = (3 - blk, dp)
        greet((*summed.place[6:], diagonal))

    def vec(row):
        return vec_ref[row : row + 1]

    vec_grad_ref[...] = jnp.zeros_like(vec_grad_ref)
    loads[0].wait()

    @pl.loop(0, count // strip)
    def _(at):
        rows = pl.ds(pl.multiple_of(at * strip, strip), strip)
        hidden[rows, :] = (normed[rows, :] * vec(8) + vec(9)).astype(low)

    def widen(part, pre):
        load_wide(part).wait()
        pre[...] = contract_cols(hidden[...], w_inner[columns(part), :])

    per_row = D // chunk

    def bend(part, pre):
        bias = vec_ref[pl.ds(3 + part // per_row, 1), :]
        side = lax.rem(part, per_row)
        piece = bias[:, 0:chunk]
        for other in range(1, per_row):
            piece = jnp.where(side == other, bias[:, other * chunk : (other + 1) * chunk], piece)
        for at in range(0, count, strip):
            value, pull = gelu_pair(pre[at : at + strip] + piece)
            active[at : at + strip, columns(part)] = value.astype(low)
            slope[at : at + strip, columns(part)] = pull

    widen(0, left_pre)

    @pl.loop(0, chunks // 2 - 1)
    def _(turn):
        widen(2 * turn + 1, right_pre)
        bend(2 * turn, left_pre)
        widen(2 * turn + 2, left_pre)
        bend(2 * turn + 1, right_pre)

    widen(chunks - 1, right_pre)
    bend(chunks - 2, left_pre)
    bend(chunks - 1, right_pre)

    for load in loads[1:4]:
        load.wait()
    passages = lengths_ref.shape[0] // lax.axis_size("blk")
    per_passage = count // passages

    def put_tile(at, value):
        rows = slice(at % 2 * tile, (at % 2 + 1) * tile)
        left_pre[rows] = value[:, 0:chunk]
        right_pre[rows] = value[:, chunk:]

    def get_strip(at, inner_at):
        first = at % 2 * tile + inner_at
        rows = slice(first, first + strip)
        return jnp.concatenate([left_pre[rows], right_pre[rows]], axis=1)

    def narrow(at):
        return jnp.dot(active[at * tile : (at + 1) * tile], w_outer[...], preferred_element_type=f32)

    def sums(totals, values):
        return [
            total + jnp.sum(value, axis=0, keepdims=True) for total, value in zip(totals, values)
        ]

    nothing = [jnp.zeros((1, D), f32)] * 3
    totals = nothing
    for at in range(tiles):
        put_tile(at, narrow(at))
        passage = at * tile // per_passage
        length = lengths_ref[lax.axis_index("blk") * passages + passage]
        for inner_at in range(0, tile, strip):
            first = at * tile + inner_at
            rows = slice(first, first + strip)
            mixed = normed[rows] * vec(8) + vec(9) + (
                get_strip(at, inner_at) + vec(7)
            )
            normed_two, inv_two = norm_rows(mixed)
            local = first - passage * per_passage
            output[passage, local : local + strip] = (normed_two * vec(10) + vec(11)).astype(low)
            position = local + lax.broadcasted_iota(
                jnp.int32, (strip, 1), 0
            )
            grad_out = jnp.where(position < length, cot[rows].astype(f32), 0.0)
            d_mixed_two = norm_back(grad_out * vec(10), normed_two, inv_two)
            d_mixed[rows] = d_mixed_two
            low_branch = d_mixed_two.astype(low)
            d_branch[rows] = low_branch
            totals = sums(totals, (grad_out * normed_two, grad_out, low_branch.astype(f32)))
    for row, total in zip((10, 11, 7), totals):
        vec_grad_ref[row : row + 1] = total
    if beside:
        blk = lax.axis_index("blk")
        pl.semaphore_wait(pltpu.get_barrier_semaphore(), 4)
        span = output_ref.shape[1]
        there = output_ref.at[pl.ds(blk * passages, passages)]
        given = [
            remote_copy(output.at[:, pl.ds(peer[0] * span, span)], there, swap_sem, slot, peer)
            for slot, peer in enumerate((*summed.place[7:], diagonal))
        ]
        own_piece = output.at[:, pl.ds(blk * span, span)]
        given.append(pltpu.make_async_copy(own_piece, there, done_sem.at[0]))
    else:
        given = [pltpu.make_async_copy(output, output_ref, done_sem.at[0])]
    for copy in given:
        copy.start()

    order = plane_order(chunks)

    def store(turn, side):
        part, slot = order(turn), lax.rem(turn, 2)
        if side == 0:
            return pltpu.make_async_copy(
                staged_outer.at[slot], d_outer_ref.at[part], store_sem.at[slot, 0]
            )
        rows = pl.ds(part * chunk, chunk)
        return pltpu.make_async_copy(staged.at[slot], d_inner_ref.at[rows], store_sem.at[slot, 1])

    tasks = {}
    if beside:

        tasks = {
            2: lambda: summed.begin([0]),
            4: lambda: (summed.paired([0]), summed.begin([1])),
            6: lambda: (summed.paired([1]), summed.begin([2])),
        }

    @pl.loop(0, chunks)
    def _(turn):
        part, slot = order(turn), lax.rem(turn, 2)
        cols = columns(part)
        left_pre[...] = contract_cols(d_branch[...], w_outer[cols, :])
        outer_rows = contract_rows(active[:, cols], d_branch[...]).astype(low)
        staged_outer[slot] = outer_rows.reshape(staged_outer.shape[1:])
        total = jnp.zeros((1, chunk), f32)
        for at in range(0, count, strip):
            d_pre = (left_pre[at : at + strip] * slope[at : at + strip, cols]).astype(low)
            active[at : at + strip, cols] = d_pre
            total = total + jnp.sum(d_pre.astype(f32), axis=0, keepdims=True)
        bias_row = pl.ds(3 + part // per_row, 1)
        side_at = lax.rem(part, per_row)
        for other in range(per_row):
            lanes = slice(other * chunk, (other + 1) * chunk)
            vec_grad_ref[bias_row, lanes] += jnp.where(side_at == other, total, 0.0)
        staged[slot] = contract_rows(active[:, cols], hidden[...]).astype(low)
        for side in range(2):
            store(turn, side).start()

        @pl.when(turn >= 1)
        def _():
            for side in range(2):
                store(turn - 1, side).wait()

        for at in sorted(tasks):
            run_when(turn == at, tasks[at])

    for side in range(2):
        store(chunks - 1, side).wait()
    if beside:
        summed.begin([3])
        summed.paired([2])
    loads[5].start()
    loads[4].wait()
    ctx, d_attn, d_ctx = hidden, d_branch, cot
    totals = nothing
    for at in range(tiles):
        span = slice(at * tile, (at + 1) * tile)
        put_tile(at, jnp.dot(active[span], w_inner[...], preferred_element_type=f32))
        for inner_at in range(0, tile, strip):
            first = at * tile + inner_at
            rows = slice(first, first + strip)
            d_hidden = d_mixed[rows] + get_strip(at, inner_at)
            normed_one = normed[rows]
            d_mixed_one = norm_back(d_hidden * vec(8), normed_one, inv_std[rows, 0:1])
            d_mixed[rows] = d_mixed_one
            low_attn = d_mixed_one.astype(low)
            d_attn[rows] = low_attn
            totals = sums(totals, (d_hidden * normed_one, d_hidden, low_attn.astype(f32)))
        d_ctx[span] = contract_cols(d_attn[span], w_out[...]).astype(low)
        if beside and at == 0:
            summed.paired([3])
        if beside and at == 2:
            summed.half_settled([0, 1], red_ref, red_sem)
    for row, total in zip((8, 9, 2), totals):
        vec_grad_ref[row : row + 1] = total
    results = [
        pltpu.make_async_copy(d_ctx, d_ctx_ref, done_sem.at[1]),
        pltpu.make_async_copy(d_mixed, d_mixed_ref, done_sem.at[2]),
    ]
    for copy in results:
        copy.start()
    half = staged.shape[1]
    loads[5].wait()
    for side in range(2):
        rows = slice(side * half, (side + 1) * half)
        staged[side] = contract_rows(ctx[:, rows], d_attn[...]).astype(low)
        copy = pltpu.make_async_copy(staged.at[side], d_out_ref.at[rows], done_sem.at[3 + side])
        copy.start()
        results.append(copy)
    if beside:
        summed.half_settled([2, 3], red_ref, red_sem)
        results += [summed.kept(slot, red_ref, red_sem) for slot in range(4)]
    for copy in given + results:
        copy.wait()


def ffn(lengths, normed, inv_std, cotangent, context, vec_rows, table, passages, beside):
    f32, low = jnp.float32, jnp.bfloat16
    count = normed.shape[0]
    shares = (4 * passages, count // passages // 4) if beside else (passages, count // passages)
    chunk = 8 * GRAIN
    any_spec = pl.BlockSpec(memory_space=pl.ANY)
    vmem = pl.BlockSpec(memory_space=pltpu.VMEM)
    dma = pltpu.SemaphoreType.DMA
    whole = lambda width, kind=low: pltpu.VMEM((count, width), kind)
    granules = FF // chunk
    more_shape, more, extra = (), [], {}
    if beside:
        more_shape = (jax.ShapeDtypeStruct((granules, 2, GRAIN, D), low),)
        more = PlaneSum.scratch(OUTER_COUNTS, with_part=False)
        more[3] = pltpu.VMEM((1, GRAIN, D), low)
        more += [dma((4,)), dma((2, 3))]
        extra = dict(collective_id=4, has_side_effects=True)
    return pl.pallas_call(
        ffn_kernel,
        out_shape=(
            jax.ShapeDtypeStruct((*shares, D), low),
            jax.ShapeDtypeStruct((count, D), f32),
            jax.ShapeDtypeStruct((count, D), low),
            jax.ShapeDtypeStruct((VEC_LEN // D, D), f32),
            jax.ShapeDtypeStruct((D, D), low),
            jax.ShapeDtypeStruct((FF, D), low),
            jax.ShapeDtypeStruct((granules, 2, 2, 2, GRAIN, D), low),
        )
        + more_shape,
        in_specs=[pl.BlockSpec(memory_space=pltpu.SMEM), vmem] + [any_spec] * 5,
        out_specs=(any_spec, any_spec, any_spec, vmem)
        + (any_spec,) * (3 + len(more_shape)),
        scratch_shapes=[
            pltpu.VMEM((D, D), low),
            pltpu.VMEM((FF, D), low),
            pltpu.VMEM((FF, D), low),
            whole(D, f32),
            whole(128, f32),
            whole(D),
            whole(chunk, f32),
            whole(chunk, f32),
            whole(FF, f32),
            whole(FF),
            whole(D),
            pltpu.VMEM((passages, count // passages, D), low),
            whole(D),
            whole(D, f32),
            pltpu.VMEM((2, chunk, D), low),
            pltpu.VMEM((2, 2, 2, 2, GRAIN, D), low),
            dma((6,)),
            dma((2, 2)),
            dma((5,)),
            dma((granules,)),
        ]
        + more,
        compiler_params=pltpu.CompilerParams(vmem_limit_bytes=63 * 1024 * 1024, **extra),
        cost_estimate=pl.CostEstimate(
            flops=count * (12 * D * FF + 4 * D * D),
            bytes_accessed=2 * (14 * D * D + 14 * D * count),
            transcendentals=count * FF,
        ),
        name="ffn",
    )(lengths, vec_rows, normed, inv_std, cotangent, context, table)


def paired(own_rows, dp_count, blk_count):
    return blk_count == 4 and dp_count % 2 == 0 and own_rows % 384 == 0


def swap_in(rows):
    return lax.all_to_all(rows, "blk", split_axis=0, concat_axis=1, tiled=True)


def swap_out(rows):
    return lax.all_to_all(rows, "blk", split_axis=1, concat_axis=0, tiled=True)


def pick_blocks(blocks, order):
    return jnp.concatenate(
        [lax.dynamic_index_in_dim(blocks, order[i], 0) for i in range(blocks.shape[0])], axis=0
    )


def body(
    tokens,
    cotangent,
    lengths,
    owners,
    master,
    moment_one,
    moment_two,
    vectors,
    vector_one,
    vector_two,
):
    dp_count = lax.axis_size("dp")
    blk_count = lax.axis_size("blk")
    blk = lax.axis_index("blk")
    own_rows = master.shape[0]
    grain = math.gcd(own_rows, D)
    part = grain // blk_count
    own_grains = own_rows // grain
    fast = paired(own_rows, dp_count, blk_count)
    if fast:
        full = own_rows * 2 // 9
        tokens, cotangent, table, *attended, vec_rows = enter(
            dp_count // 2, full, owners, tokens, cotangent, master, lengths, vectors
        )
    else:
        own_part = lax.dynamic_index_in_dim(
            master.reshape(own_grains, blk_count, part, D), blk, 1, keepdims=False
        ).astype(jnp.bfloat16)
        part_blocks = lax.all_gather(own_part, "dp", axis=0)
        part_table = pick_blocks(part_blocks, jnp.argsort(owners)).reshape(dp_count * own_grains, part, D)
        tokens = swap_in(tokens)
        cotangent = swap_in(cotangent)

        rows = lax.all_gather(part_table, "blk", axis=1)
        table = rows.reshape(-1, D)
        vec_rows = vectors.reshape(-1, D)
        attended = attend(lengths, tokens, table, vec_rows)
    queries, keys, values, log_total, context, normed_one, inv_one = attended
    passages, span_len, _ = tokens.shape
    tok_rows = passages * span_len
    flat = lambda rows: rows.reshape(tok_rows, -1)
    output, d_mixed_one, d_context, grad_vector, d_w_out, d_w_inner, d_w_outer, *outer_red = ffn(
        lengths,
        flat(normed_one),
        flat(inv_one),
        flat(cotangent),
        flat(context),
        vec_rows,
        table,
        passages,
        fast,
    )
    split = lambda g: g.reshape(-1, 2, 2, 2, GRAIN, D)
    d_tokens, d_w_qkv, grad_vector, *back = attend_back(
        lengths,
        tokens,
        table,
        queries,
        keys,
        values,
        log_total,
        d_context.reshape(passages, span_len, D),
        d_mixed_one.reshape(passages, span_len, D),
        grad_vector,
        [split(d_w_out), split(d_w_inner), *outer_red] if fast else (),
    )

    def own_parts(rows):
        split = rows.astype(jnp.bfloat16).reshape(-1, blk_count, part, D)
        return lax.psum_scatter(split, "blk", scatter_dimension=1)

    if fast:
        own_block, vector_sum, norms, grad_tokens = tail(
            dp_count // 2, owners, split(d_w_qkv), back[0], grad_vector, d_tokens
        )
        grad_norm = norms[0, 0]
        vector_sum = vector_sum.reshape(-1)
        own_block = own_block.reshape(own_rows, D)
    else:
        output, grad_tokens = swap_out(output), swap_out(d_tokens)
        part_grads = jnp.concatenate(
            [own_parts(d_w_qkv), own_parts(d_w_out), own_parts(d_w_inner), own_parts(d_w_outer.reshape(FF, D))],
            axis=0,
        )
        ordered = pick_blocks(part_grads.reshape(dp_count, own_grains, part, D), owners)
        own_grad = lax.psum_scatter(ordered, "dp", scatter_dimension=0)
        own_f32 = own_grad.astype(jnp.float32)
        own_block = lax.all_gather(own_grad, "blk", axis=1).reshape(own_rows, D)
        vector_sum = lax.psum(grad_vector, ("dp", "blk"))
        squares = lax.psum(jnp.sum(own_f32 * own_f32), ("dp", "blk"))
        vector_sum = vector_sum.reshape(-1)
        grad_norm = jnp.sqrt(squares + jnp.sum(vector_sum * vector_sum))
    factor = jnp.minimum(1.0, clip_norm / (grad_norm + 1e-06))
    own_grad = own_block.astype(jnp.float32) * factor
    new_vectors, new_vone, new_vtwo = adamw(
        vectors, vector_one, vector_two, vector_sum * factor, 0.0, vector_rate
    )
    new_master, new_one, new_two = adamw(
        master, moment_one, moment_two, own_grad, weight_decay, learn_rate
    )
    return (
        output,
        grad_tokens,
        grad_norm,
        new_master,
        new_one,
        new_two,
        new_vectors,
        new_vone,
        new_vtwo,
    )


def solution(mesh):
    in_specs = (
        P("dp", "blk", None),
        P("dp", "blk", None),
        P("dp"),
        P(),
        P("dp", None),
        P("dp", None),
        P("dp", None),
        P(),
        P(),
        P(),
    )
    out_specs = (
        P("dp", "blk", None),
        P("dp", "blk", None),
        P(),
        P("dp", None),
        P("dp", None),
        P("dp", None),
        P(),
        P(),
        P(),
    )
    return jax.shard_map(body, mesh=mesh, in_specs=in_specs, out_specs=out_specs, check_vma=False)
```

time: 1120 us -> 293 us (0.26)
  waiting for transfers between devices: 637 us -> 0 us
  Pallas kernels: 0 us -> 272 us
  matrix products: 223 us -> 0 us
  local copies, waits for them, and re-layouts: 89.4 us -> 3.12 us
  other arithmetic: 92.7 us -> 10.7 us
  blocking collectives: 47.5 us -> 0 us
  between operations: 17.5 us -> 3.49 us
    reduce_scatter x3 -> x0, waiting for transfers between devices: 370 us -> none  [the longest x1 277 us: body(): lax.psum_scatter(ordered.reshape(-1, D), 'dp', scatter_dimension=0, tiled...]
    pallas_call x0 -> x4, Pallas kernels: none -> 272 us  [the longest x1 86.2 us: enter(): pl.pallas_call(functools.partial(enter_kernel, nz, full), out_shape=(shap...]
    all_gather x3 -> x0, waiting for transfers between devices: 232 us -> none  [the longest x1 131 us: body(): lax.all_gather(master.astype(jnp.bfloat16), 'dp', axis=0, tiled=True)]
    dot_general x24 -> x0, matrix products: 223 us -> none  [the longest x6 76.5 us: contract_cols(): lax.dot_general(left, right, (((1,), (1,)), ((), ())), preferred_element_...]
    psum x2 -> x0, blocking collectives: 47.5 us -> none  [the longest x1 30.1 us: body(): lax.psum((vector_part, jnp.sum(own_block * own_block)), 'dp')]
    psum x1 -> x0, waiting for transfers between devices: 34.3 us -> none  [body(): lax.psum(own_partial.astype(jnp.bfloat16), 'blk').astype(jnp.float32)]
    gather x2 -> x0, local copies, waits for them, and re-layouts: 32.8 us -> none  [the longest x1 20.7 us: body(): jnp.take(grad_table.reshape(dp_count, own_rows, D), owners, axis=0)]
    select_n x4 -> x0, other arithmetic: 31.5 us -> none  [the longest x2 22.3 us: body(): jnp.take(grad_table.reshape(dp_count, own_rows, D), owners, axis=0)]
  transfers between devices with their start and end apart: 7 -> 0, of which waited for: 7 -> 0; matrix products, arithmetic and copies ran while one was open for 9% -> 0% of each run, Pallas kernels for 0% -> 0%
where the time goes in v1:
time: 293 us; the launch traced here: 289 us
  Pallas kernels  272 us (93%)
  other arithmetic  10.7 us (4%)
  between operations  3.49 us (1%)
  local copies, waits for them, and re-layouts  3.12 us (1%)
    pallas_call x1, Pallas kernels, enter(): pl.pallas_call(functools.partial(enter_kernel, nz, full), out_shape=(shap...  86.2 us
    pallas_call x1, Pallas kernels, tail(): pl.pallas_call(functools.partial(tail_kernel, nz), out_shape=(jax.ShapeDt...  76 us
    pallas_call x1, Pallas kernels, ffn(): pl.pallas_call(ffn_kernel, out_shape=(jax.ShapeDtypeStruct((*shares, D),...  62.5 us
    pallas_call x1, Pallas kernels, attend_back(): pl.pallas_call(attend_back_kernel, grid=(passages,), out_shape=(jax.Shape...  46.9 us
    sub x2, other arithmetic, adamw(): return (weight - rate * (direction + decay * weight), new_first, new_second)  8.84 us

profile of v1, /device:TPU:0, one launch (start us, length us, event | category | flops | bytes accessed | tf_op | source)
XLA Modules:
  0.0 288.9 jit_solution(2193636128333843515)
XLA Ops:
  0.6 86.2 %enter.1 = (bf16[2,512,768]{2,1,0:T(8,128)(2,1)}, bf16[2,512,768]{2,1,0:T(8,128)(2,1)}, bf16[9216,768]{1,0:T(8,128)(2,1)}, bf16[2,512,768]{2,1,0:T(8,128)(2,1)},...) custom-call(s32[8]{0:T(128)} %owners_ref.3, ...), custom_call_target="tpu_custom_call" | custom-call | flops 6442450944 | bytes 60000000 | tf_op jit(solution)/shard_map/enter/pallas_call | solution.py:458
  86.9 62.5 %ffn.1 = (bf16[8,128,768]{2,1,0:T(8,128)(2,1)}, f32[1024,768]{1,0:T(8,128)}, bf16[1024,768]{1,0:T(8,128)(2,1)}, f32[12,768]{1,0:T(8,128)}, bf16[768,768]{1,0:T(8...) custom-call(s32[8]{0:T(128)} %lengths_ref.5, ...), custom_call_target="tpu_custom_call" | custom-call | flops 31406948352 | bytes 38535168 | tf_op jit(solution)/shard_map/ffn/pallas_call | solution.py:1726
  149.4 46.9 %attend_back.1 = (bf16[2,512,768]{2,1,0:T(8,128)(2,1)}, bf16[2304,768]{1,0:T(8,128)(2,1)}, f32[12,768]{1,0:T(8,128)}, bf16[18,48,768]{2,1,0:T(8,128)(2,1)}) custom-call(s32[8]{0:T(128)} %lengths_ref.5, bf16[2,512,768]{2,1,0:T(8,128)(2,1)} %get-tuple-element.42.x_ref, bf16[9216,768]{1,0:T(8,128)(2,1)} %get-tuple-element.40.table_ref.w_ref, ...), custom_call_target="tpu_custom_call" | custom-call | flops 11274289152 | bytes 18874368 | tf_op jit(solution)/shard_map/attend_back/pallas_call | solution.py:1353
  196.3 76.0 %grad_tail.1 = (bf16[3,2,2,2,48,768]{5,4,3,2,1,0:T(8,128)(2,1)}, f32[72,128]{1,0:T(8,128)}, f32[1,1]{1,0:T(1,128)}, bf16[8,128,768]{2,1,0:T(8,128)(2,1)}) custom-call(s32[8]{0:T(128)} %owners_ref.3, bf16[6,2,2,2,48,768]{5,4,3,2,1,0:T(8,128)(2,1)} %bitcast.21, bf16[18,48,768]{2,1,0:T(8,128)(2,1)} %get-tuple-element.54.back_ref, ...), custom_call_target="tpu_custom_call" | custom-call | flops 10000000 | bytes 30000000 | tf_op jit(solution)/shard_map/grad_tail/pallas_call | solution.py:769
  272.2 0.0 copy-start
  273.1 1.7 multiply_subtract_fusion.1
  274.7 1.9 convert_multiply_fusion
  276.6 0.0 copy-done
  276.6 0.0 copy-start.1
  276.6 7.2 %multiply_subtract_fusion = (f32[1152,768]{1,0:T(8,128)}, f32[1152,768]{1,0:T(8,128)}, f32[1152,768]{1,0:T(8,128)}) fusion(f32[1152,768]{1,0:T(8,128)S(1)} %copy-done, f32[3,2,2,2,48,768]{5,4,3,2,1,0:T(8,128)S(1)} %convert_multiply_fusion, f32[1152,768]{1,0:T(8,128)} %param.15, f32[1152,768]{1,0:T(8,128)} %param.16), kind=kLoop, calls=%fused_computation.3 | loop fusion | flops 12386304 | bytes 24772608 | tf_op jit(solution)/shard_map/sub | solution.py:54
  283.8 0.0 copy-start.2
  283.8 0.0 copy-done.1
  283.8 1.1 copy.22
  285.0 0.8 copy-done.2
  285.8 1.1 copy.23
Async XLA Ops:
  272.2 4.4 %copy-start = (f32[1152,768]{1,0:T(8,128)S(1)}, f32[1152,768]{1,0:T(8,128)}, u32[]{:S(2)}) copy-start(f32[1152,768]{1,0:T(8,128)} %master_ref.1) | copy-start | bytes 10616836
  276.6 7.2 %copy-start.1 = (bf16[8,128,768]{2,1,0:T(8,128)(2,1)S(1)}, bf16[8,128,768]{2,1,0:T(8,128)(2,1)}, u32[]{:S(2)}) copy-start(bf16[8,128,768]{2,1,0:T(8,128)(2,1)} %get-tuple-element.76) | copy-start | bytes 4718596
  283.8 2.0 copy-start.2

commit v2 on v1

--- a/solution.py
+++ b/solution.py
@@ -526,13 +526,11 @@
     norm_ref,
     d_tokens_out,
     acc,
-    core_land,
     land_one,
     land_two,
-    load_sem,
-    core_sem,
     one_sem,
     two_sem,
+    late_sem,
     part,
     mine,
     up_land,
@@ -572,15 +570,19 @@
     late = qkv_ref.shape[0]
     load = pltpu.make_async_copy(back_ref, part.at[pl.ds(late, back_ref.shape[0])], part_sem)
     load.start()
-    sems = (load_sem, core_sem, one_sem, two_sem)
-    summed = PlaneSum((qkv_ref,), QKV_COUNTS, acc, core_land, land_one, land_two, part, sems)
+    late_load = pltpu.make_async_copy(qkv_ref, acc, late_sem)
+    late_load.start()
+    sems = (None, None, one_sem, two_sem)
+    summed = PlaneSum((), QKV_COUNTS, acc, None, land_one, land_two, part, sems)
     slots = range(len(summed.chunks))
     for row in range(VEC_LEN // D):
         for col in range(D // 128):
             at = row * (D // 128) + col
             vec_send[0, at : at + 1] = vec_ref[row : row + 1, col * 128 : (col + 1) * 128]
+    late_load.wait()
     pl.semaphore_wait(barrier, len(partners))
-    summed.begin(slots)
+    for slot in slots:
+        summed.one(slot).start()
 
     def vec_copy(turn):
         peer = (sibling, x_peer, y_peer)[turn]
@@ -593,7 +595,6 @@
             vec_copy(turn + 1).start()
 
     vec_copy(0).start()
-    summed.paired(slots)
     vec_next(0)
     vec_next(1)
     vec_next(2)
@@ -747,8 +748,16 @@
     for piece in range(grains):
         gather(3, piece).wait()
         gather(4, piece).wait()
-        done.append(pltpu.make_async_copy(assembled.at[piece], own_ref.at[piece], out_sem.at[piece]))
-        done[-1].start()
+        for place in range(8):
+            at = (piece * 8 + place) * GRAIN
+            done.append(
+                pltpu.make_async_copy(
+                    assembled.at[piece, place // 4, place // 2 % 2, place % 2],
+                    own_ref.at[pl.ds(at, GRAIN)],
+                    out_sem.at[piece, place],
+                )
+            )
+            done[-1].start()
     for swap in swaps:
         swap.end()
     for copy in done:
@@ -759,7 +768,8 @@
     low, f32 = jnp.bfloat16, jnp.float32
     passages, span, _ = d_tokens.shape
     swapped = jax.ShapeDtypeStruct((4 * passages, span // 4, D), low)
-    granules = g_qkv.shape[0] + back.shape[0]
+    late = g_qkv.shape[0]
+    granules = late + back.shape[0]
     grains = granules // (2 * nz)
     any_spec = pl.BlockSpec(memory_space=pl.ANY)
     vmem = pl.BlockSpec(memory_space=pltpu.VMEM)
@@ -769,7 +779,7 @@
     return pl.pallas_call(
         functools.partial(tail_kernel, nz),
         out_shape=(
-            jax.ShapeDtypeStruct((grains, 2, 2, 2, GRAIN, D), low),
+            jax.ShapeDtypeStruct((grains * 8 * GRAIN, D), low),
             jax.ShapeDtypeStruct(lanes, f32),
             jax.ShapeDtypeStruct((1, 1), f32),
             swapped,
@@ -778,8 +788,13 @@
         + [any_spec] * 2
         + [vmem, any_spec],
         out_specs=(any_spec, vmem, vmem, any_spec),
-        scratch_shapes=PlaneSum.scratch(QKV_COUNTS, with_part=False)
-        + [
+        scratch_shapes=[
+            block(late, 2, 2),
+            block(late, 2),
+            block(late),
+            dma((2, len(plane_chunks(QKV_COUNTS)))),
+            dma((2, len(plane_chunks(QKV_COUNTS)))),
+            dma(()),
             block(granules),
             block(2 * nz, grains),
             block(nz, grains, 2),
@@ -798,7 +813,7 @@
             dma((2, 5 * grains)),
             dma((2, 2 + nz)),
             dma((2, 2 + nz)),
-            dma((grains,)),
+            dma((grains, 8)),
         ]
         + PositionSwap.scratch(passages, span),
         compiler_params=pltpu.CompilerParams(
@@ -1062,7 +1077,7 @@
             self.load(slot).start()
             self.core(slot).start()
 
-    def paired(self, slots):
+    def paired(self, slots, go_on=True):
         for slot in slots:
             self.load(slot).wait()
             self.core(slot).wait()
@@ -1072,7 +1087,8 @@
             def _(g):
                 self.acc[g] = add_low(self.acc[g], self.core_land[g])
 
-            self.one(slot).start()
+            if go_on:
+                self.one(slot).start()
 
     def crossed(self, slots):
         _, _, _, _, y, x, _, _, _ = self.place
@@ -1239,14 +1255,16 @@
     *refs,
 ):
     f32, low = jnp.float32, jnp.bfloat16
-    beside = len(refs) > 9
+    beside = len(refs) > 13
     tasks = {}
     if beside:
         *sources, outer_red, refs = *refs[:3], refs[3:]
         red_ref, refs = refs[3], refs[:3] + refs[4:]
-        extra, refs = refs[9:], refs[:9]
-        acc, core_land, one_land, two_land, *sems, keep, land, keep_sem, keep_two, share, red_sem = extra
-    grad_ref, table_ref, vec_ref, k_turned, dq_turned, dq_all, dk_all, dv_all, x_all = refs
+        extra, refs = refs[13:], refs[:13]
+        acc, core_land, one_land, two_land, *sems, keep, land, keep_sem, keep_two, share, red_sem = extra[:14]
+        late, late_acc, late_land, late_load, late_core, late_sem = extra[14:]
+    grad_ref, table_ref, vec_ref, k_turned, dq_turned, dq_all, dk_all, dv_all, x_all = refs[:9]
+    scores, d_probs, probs_low, d_scores = refs[9:]
     passage = pl.program_id(0)
     if beside:
         summed = PlaneSum(sources, BACK_COUNTS, acc, core_land, one_land, two_land, share, sems)
@@ -1254,6 +1272,9 @@
             outer_red, OUTER_COUNTS, keep, land, share, keep_sem, keep_two, sum(BACK_COUNTS)
         )
         slots = range(len(summed.chunks))
+        late_sems = (late_load, late_core, None, None)
+        late_sum = PlaneSum((late,), QKV_COUNTS, late_acc, late_land, None, None, None, late_sems)
+        late_slots = range(len(late_sum.chunks))
 
         @pl.when(passage == 0)
         def _():
@@ -1273,18 +1294,20 @@
 
         def end():
             summed.settled(slots)
-            stored = pltpu.make_async_copy(share, red_ref, red_sem)
-            stored.start()
-            stored.wait()
+            stored = [pltpu.make_async_copy(share, red_ref, red_sem)]
+            stored[0].start()
+            late_sum.paired(late_slots, go_on=False)
+            stored.append(pltpu.make_async_copy(late_acc, table_ref, late_sem))
+            stored[1].start()
+            for copy in stored:
+                copy.wait()
 
     span = x_ref.shape[1]
-    half_span = span // 2
+    half_span, strip = span // 2, 64
     length = lengths_ref[lax.axis_index("blk") * pl.num_programs(0) + passage]
     rows = pl.ds(pl.multiple_of(passage * span, span), span)
     x_all[rows, :] = x_ref[0]
     k_turned[...] = k_ref[0].astype(f32).T.astype(low)
-    valid = lax.broadcasted_iota(jnp.int32, (span, half_span), 0) < length
-
     @pl.loop(0, HEADS // 2)
     def _(pair):
         slot = passage * (HEADS // 2) + pair
@@ -1293,30 +1316,61 @@
         lanes = pl.ds(pl.multiple_of(pair * 128, 128), 128)
         keys, values = k_ref[0, :, lanes], v_ref[0, :, lanes]
         dk, dv = jnp.zeros((span, 128), f32), jnp.zeros((span, 128), f32)
-        for half in range(2):
-            head_keys, head_values = keep_lanes(keys, half), keep_lanes(values, half)
+        units = [(half, part) for half in range(2) for part in range(2)]
+
+        def products(unit):
+            half, part = units[unit]
+            cols = pl.ds(part * half_span, half_span)
+            scores[unit % 2] = contract_cols(keep_lanes(keys, half), q_ref[0, cols, lanes])
+            d_probs[unit % 2] = contract_cols(keep_lanes(values, half), d_ctx_ref[0, cols, lanes])
+
+        def fold(value):
+            return jnp.sum(value.reshape(strip // 8, 8, half_span), axis=0)
+
+        products(0)
+        for unit, (half, part) in enumerate(units):
+            if unit + 1 < len(units):
+                products(unit + 1)
+            cols = pl.ds(part * half_span, half_span)
+            side = unit % 2
+            log_total = lse_ref[0, 2 * pair + half, :, cols]
+            sums = jnp.zeros((8, half_span), f32)
+            for at in range(0, span, strip):
+                here = slice(at, at + strip)
+                row = at + lax.broadcasted_iota(jnp.int32, (strip, half_span), 0)
+                masked = jnp.where(row < length, scores[side, here], -1000000000.0)
+                probs = jnp.exp(masked - log_total)
+                weighted = probs * d_probs[side, here]
+                probs_low[side, here] = probs.astype(low)
+                scores[side, here] = probs
+                d_probs[side, here] = weighted
+                sums = sums + fold(weighted)
+            inner = jnp.sum(sums, axis=0, keepdims=True)
+            for at in range(0, span, strip):
+                here = slice(at, at + strip)
+                d_scores[side, here] = (d_probs[side, here] - scores[side, here] * inner).astype(low)
+            d_out = keep_lanes(d_ctx_ref[0, cols, lanes], half)
+            dv = dv + jnp.dot(probs_low[side], d_out, preferred_element_type=f32)
+            queries = keep_lanes(q_ref[0, cols, lanes], half)
+            dk = dk + jnp.dot(d_scores[side], queries, preferred_element_type=f32)
             turned = k_turned[pl.ds(pl.multiple_of(pair * 128 + half * 64, 64), 64), :]
-            for part in range(2):
-                cols = pl.ds(part * half_span, half_span)
-                queries = q_ref[0, cols, lanes]
-                d_out = d_ctx_ref[0, cols, lanes]
-                scores = contract_cols(head_keys, queries)
-                scores = jnp.where(valid, scores, -1000000000.0)
-                probs = jnp.exp(scores - lse_ref[0, 2 * pair + half, :, cols])
-                dv = dv + jnp.dot(
-                    probs.astype(low), keep_lanes(d_out, half), preferred_element_type=f32
-                )
-                d_probs = contract_cols(head_values, d_out)
-                weighted = probs * d_probs
-                inner = jnp.sum(weighted, axis=0, keepdims=True)
-                d_scores = (weighted - probs * inner).astype(low)
-                dk = dk + jnp.dot(d_scores, keep_lanes(queries, half), preferred_element_type=f32)
-                dq_turned[half * 64 : half * 64 + 64, cols] = (
-                    jnp.dot(turned, d_scores, preferred_element_type=f32) * 0.125
-                )
+            dq_turned[half * 64 : half * 64 + 64, cols] = (
+                jnp.dot(turned, d_scores[side], preferred_element_type=f32) * 0.125
+            )
         dq_all[rows, lanes] = dq_turned[...].T.astype(low)
         dk_all[rows, lanes] = dk.astype(low)
         dv_all[rows, lanes] = dv.astype(low)
+
+    @pl.when(passage == pl.num_programs(0) - 1)
+    def _():
+        for at, part in enumerate((dq_all, dk_all, dv_all)):
+            d_weight = contract_rows(x_all[...], part[...]).astype(low)
+            if beside:
+                late[2 * at : 2 * at + 2] = d_weight.reshape(2, 2, 2, 2, GRAIN, D)
+                if at >= 1:
+                    late_sum.begin([at - 1])
+            else:
+                table_ref[at * D : (at + 1) * D] = d_weight
 
     grad = d_mixed_ref[0]
     for lo, part in ((0, dq_all), (D, dk_all), (2 * D, dv_all)):
@@ -1325,13 +1379,11 @@
 
     @pl.when(passage == pl.num_programs(0) - 1)
     def _():
-        for lo, part in ((0, dq_all), (D, dk_all), (2 * D, dv_all)):
-            table_ref[lo : lo + D] = contract_rows(x_all[...], part[...]).astype(low)
-        if beside:
-            end()
         vec_ref[...] = vec_in_ref[...]
         vec_ref[0:1] = jnp.sum(dq_all[...].astype(f32), axis=0, keepdims=True)
         vec_ref[1:2] = jnp.sum(dv_all[...].astype(f32), axis=0, keepdims=True)
+        if beside:
+            end()
 
 
 def attend_back(
@@ -1343,11 +1395,25 @@
     whole = pltpu.VMEM((passages * span, D), low)
     any_spec = pl.BlockSpec(memory_space=pl.ANY)
     red_shape, beside, extra, more = (), [], {}, ()
+    table_shape = jax.ShapeDtypeStruct((3 * D, D), low)
+    table_spec = pl.BlockSpec((3 * D, D), lambda p: (0, 0))
     if sources:
         total = sum(BACK_COUNTS) + sum(OUTER_COUNTS)
         red_shape = (jax.ShapeDtypeStruct((total, GRAIN, D), low),)
         beside = PlaneSum.scratch(BACK_COUNTS, with_part=False) + SecondStep.scratch(OUTER_COUNTS)
-        beside += [pltpu.VMEM((total, GRAIN, D), low), pltpu.SemaphoreType.DMA]
+        dma = pltpu.SemaphoreType.DMA
+        beside += [pltpu.VMEM((total, GRAIN, D), low), dma]
+        late, chunks = sum(QKV_COUNTS), len(plane_chunks(QKV_COUNTS))
+        table_shape = jax.ShapeDtypeStruct((late, 2, 2, GRAIN, D), low)
+        table_spec = any_spec
+        beside += [
+            pltpu.VMEM((late, 2, 2, 2, GRAIN, D), low),
+            pltpu.VMEM((late, 2, 2, GRAIN, D), low),
+            pltpu.VMEM((late, 2, 2, GRAIN, D), low),
+            dma((chunks,)),
+            dma((2, chunks)),
+            dma,
+        ]
         extra = dict(collective_id=3, has_side_effects=True)
         more = sources
     return pl.pallas_call(
@@ -1355,7 +1421,7 @@
         grid=(passages,),
         out_shape=(
             jax.ShapeDtypeStruct((passages, span, D), low),
-            jax.ShapeDtypeStruct((3 * D, D), low),
+            table_shape,
             jax.ShapeDtypeStruct((VEC_LEN // D, D), f32),
         )
         + red_shape,
@@ -1374,12 +1440,13 @@
         + [any_spec] * len(more),
         out_specs=(
             rows,
-            pl.BlockSpec((3 * D, D), lambda p: (0, 0)),
+            table_spec,
             pl.BlockSpec((VEC_LEN // D, D), lambda p: (0, 0)),
         )
         + (any_spec,) * len(red_shape),
         scratch_shapes=[pltpu.VMEM((D, span), low), pltpu.VMEM((128, span), f32)]
         + [whole] * 4
+        + [pltpu.VMEM((2, span, span // 2), kind) for kind in (f32, f32, low, low)]
         + beside,
         compiler_params=pltpu.CompilerParams(vmem_limit_bytes=60 * 1024 * 1024, **extra),
         cost_estimate=pl.CostEstimate(
@@ -1863,11 +1930,10 @@
 
     if fast:
         own_block, vector_sum, norms, grad_tokens = tail(
-            dp_count // 2, owners, split(d_w_qkv), back[0], grad_vector, d_tokens
+            dp_count // 2, owners, d_w_qkv, back[0], grad_vector, d_tokens
         )
         grad_norm = norms[0, 0]
         vector_sum = vector_sum.reshape(-1)
-        own_block = own_block.reshape(own_rows, D)
     else:
         output, grad_tokens = swap_out(output), swap_out(d_tokens)
         part_grads = jnp.concatenate(

time: 293 us -> 287 us (0.980)
  Pallas kernels: 272 us -> 267 us
    pallas_call x1, Pallas kernels: 76 us -> 71.2 us  [tail(): pl.pallas_call(functools.partial(tail_kernel, nz), out_shape=(jax.ShapeDt...]
where the time goes in v2:
time: 287 us; the launch traced here: 282 us
  Pallas kernels  267 us (93%)
  other arithmetic  8.99 us (3%)
  between operations  3.35 us (1%)
  local copies, waits for them, and re-layouts  3.12 us (1%)
    pallas_call x1, Pallas kernels, enter(): pl.pallas_call(functools.partial(enter_kernel, nz, full), out_shape=(shap...  86.2 us
    pallas_call x1, Pallas kernels, tail(): pl.pallas_call(functools.partial(tail_kernel, nz), out_shape=(jax.ShapeDt...  71.2 us
    pallas_call x1, Pallas kernels, ffn(): pl.pallas_call(ffn_kernel, out_shape=(jax.ShapeDtypeStruct((*shares, D),...  62.5 us
    pallas_call x1, Pallas kernels, attend_back(): pl.pallas_call(attend_back_kernel, grid=(passages,), out_shape=(jax.Shape...  46.9 us
    sub x2, other arithmetic, adamw(): return (weight - rate * (direction + decay * weight), new_first, new_second)  8.99 us

profile of v2, /device:TPU:0, one launch (start us, length us, event | category | flops | bytes accessed | tf_op | source)
XLA Modules:
  0.0 282.3 jit_solution(1981308161187463644)
XLA Ops:
  0.6 86.2 %enter.1 = (bf16[2,512,768]{2,1,0:T(8,128)(2,1)}, bf16[2,512,768]{2,1,0:T(8,128)(2,1)}, bf16[9216,768]{1,0:T(8,128)(2,1)}, bf16[2,512,768]{2,1,0:T(8,128)(2,1)},...) custom-call(s32[8]{0:T(128)} %owners_ref.3, ...), custom_call_target="tpu_custom_call" | custom-call | flops 6442450944 | bytes 60000000 | tf_op jit(solution)/shard_map/enter/pallas_call | solution.py:458
  86.9 62.5 %ffn.1 = (bf16[8,128,768]{2,1,0:T(8,128)(2,1)}, f32[1024,768]{1,0:T(8,128)}, bf16[1024,768]{1,0:T(8,128)(2,1)}, f32[12,768]{1,0:T(8,128)}, bf16[768,768]{1,0:T(8...) custom-call(s32[8]{0:T(128)} %lengths_ref.5, ...), custom_call_target="tpu_custom_call" | custom-call | flops 31406948352 | bytes 38535168 | tf_op jit(solution)/shard_map/ffn/pallas_call | solution.py:1793
  149.4 46.9 %attend_back.1 = (bf16[2,512,768]{2,1,0:T(8,128)(2,1)}, bf16[6,2,2,48,768]{4,3,2,1,0:T(8,128)(2,1)}, f32[12,768]{1,0:T(8,128)}, bf16[18,48,768]{2,1,0:T(8,128)(2,1)}) custom-call(s32[8]{0:T(128)} %lengths_ref.5, bf16[2,512,768]{2,1,0:T(8,128)(2,1)} %get-tuple-element.42.x_ref, bf16[9216,768]{1,0:T(8,128)(2,1)} %get-tuple-element.40.table_ref.w_ref, ...), custom_call_target="tpu_custom_call" | custom-call | flops 11274289152 | bytes 18874368 | tf_op jit(solution)/shard_map/attend_back/pallas_call | solution.py:1419
  196.3 0.0 copy-start
  196.3 71.2 %grad_tail.1 = (bf16[1152,768]{1,0:T(8,128)(2,1)}, f32[72,128]{1,0:T(8,128)}, f32[1,1]{1,0:T(1,128)}, bf16[8,128,768]{2,1,0:T(8,128)(2,1)}) custom-call(s32[8]{0:T(128)} %owners_ref.3, bf16[6,2,2,48,768]{4,3,2,1,0:T(8,128)(2,1)} %get-tuple-element.53.qkv_ref, bf16[18,48,768]{2,1,0:T(8,128)(2,1)} %get-tuple-element.54.back_ref, ...), custom_call_target="tpu_custom_call" | custom-call | flops 10000000 | bytes 30000000 | tf_op jit(solution)/shard_map/grad_tail/pallas_call | solution.py:779
  268.2 1.5 multiply_subtract_fusion.1
  269.7 0.0 copy-done
  269.7 0.0 copy-start.1
  269.7 7.5 %multiply_subtract_fusion = (f32[1152,768]{1,0:T(8,128)}, f32[1152,768]{1,0:T(8,128)}, f32[1152,768]{1,0:T(8,128)}) fusion(f32[1152,768]{1,0:T(8,128)S(1)} %copy-done, f32[]{:T(128)S(6)} %min.3, bf16[1152,768]{1,0:T(8,128)(2,1)} %get-tuple-element.59, f32[1152,768]{1,0:T(8,128)} %param.15, f32[1152,768]{1,0:T(8,128)} %param.16), kind=kLoop, calls=%fused_computation.3 | loop fusion | flops 14155776 | bytes 23003140 | tf_op jit(solution)/shard_map/sub | solution.py:54
  277.2 0.0 copy-start.2
  277.2 0.0 copy-done.1
  277.2 1.1 copy.22
  278.3 0.8 copy-done.2
  279.2 1.1 copy.23
Async XLA Ops:
  196.3 73.4 %copy-start = (f32[1152,768]{1,0:T(8,128)S(1)}, f32[1152,768]{1,0:T(8,128)}, u32[]{:S(2)}) copy-start(f32[1152,768]{1,0:T(8,128)} %master_ref.1) | copy-start | bytes 10616836
  269.7 7.5 %copy-start.1 = (bf16[8,128,768]{2,1,0:T(8,128)(2,1)S(1)}, bf16[8,128,768]{2,1,0:T(8,128)(2,1)}, u32[]{:S(2)}) copy-start(bf16[8,128,768]{2,1,0:T(8,128)(2,1)} %get-tuple-element.76) | copy-start | bytes 4718596
  277.2 2.0 copy-start.2

commit v3 on v2

--- a/solution.py
+++ b/solution.py
@@ -1531,7 +1531,7 @@
     count = normed.shape[0]
     chunk = left_pre.shape[1]
     chunks = FF // chunk
-    tile, strip = 256, 32
+    tile, strip = 512, 32
     tiles = count // tile
     sources = (
         (normed_ref, normed),
@@ -1748,7 +1748,7 @@
         d_ctx[span] = contract_cols(d_attn[span], w_out[...]).astype(low)
         if beside and at == 0:
             summed.paired([3])
-        if beside and at == 2:
+        if beside and at == tiles - 1:
             summed.half_settled([0, 1], red_ref, red_sem)
     for row, total in zip((8, 9, 2), totals):
         vec_grad_ref[row : row + 1] = total

time: 287 us -> 288 us (level)
  no operation moved by 1% of the time
where the time goes in v3:
time: 288 us; the launch traced here: 284 us
  Pallas kernels  268 us (93%)
  other arithmetic  8.99 us (3%)
  between operations  3.35 us (1%)
  local copies, waits for them, and re-layouts  3.12 us (1%)
    pallas_call x1, Pallas kernels, enter(): pl.pallas_call(functools.partial(enter_kernel, nz, full), out_shape=(shap...  86.2 us
    pallas_call x1, Pallas kernels, tail(): pl.pallas_call(functools.partial(tail_kernel, nz), out_shape=(jax.ShapeDt...  71.2 us
    pallas_call x1, Pallas kernels, ffn(): pl.pallas_call(ffn_kernel, out_shape=(jax.ShapeDtypeStruct((*shares, D),...  64 us
    pallas_call x1, Pallas kernels, attend_back(): pl.pallas_call(attend_back_kernel, grid=(passages,), out_shape=(jax.Shape...  47 us
    sub x2, other arithmetic, adamw(): return (weight - rate * (direction + decay * weight), new_first, new_second)  8.99 us

profile of v3, /device:TPU:0, one launch (start us, length us, event | category | flops | bytes accessed | tf_op | source)
XLA Modules:
  0.0 283.9 jit_solution(4295100128102960508)
XLA Ops:
  0.6 86.2 %enter.1 = (bf16[2,512,768]{2,1,0:T(8,128)(2,1)}, bf16[2,512,768]{2,1,0:T(8,128)(2,1)}, bf16[9216,768]{1,0:T(8,128)(2,1)}, bf16[2,512,768]{2,1,0:T(8,128)(2,1)},...) custom-call(s32[8]{0:T(128)} %owners_ref.3, ...), custom_call_target="tpu_custom_call" | custom-call | flops 6442450944 | bytes 60000000 | tf_op jit(solution)/shard_map/enter/pallas_call | solution.py:458
  86.9 64.0 %ffn.1 = (bf16[8,128,768]{2,1,0:T(8,128)(2,1)}, f32[1024,768]{1,0:T(8,128)}, bf16[1024,768]{1,0:T(8,128)(2,1)}, f32[12,768]{1,0:T(8,128)}, bf16[768,768]{1,0:T(8...) custom-call(s32[8]{0:T(128)} %lengths_ref.5, ...), custom_call_target="tpu_custom_call" | custom-call | flops 31406948352 | bytes 38535168 | tf_op jit(solution)/shard_map/ffn/pallas_call | solution.py:1793
  150.9 47.0 %attend_back.1 = (bf16[2,512,768]{2,1,0:T(8,128)(2,1)}, bf16[6,2,2,48,768]{4,3,2,1,0:T(8,128)(2,1)}, f32[12,768]{1,0:T(8,128)}, bf16[18,48,768]{2,1,0:T(8,128)(2,1)}) custom-call(s32[8]{0:T(128)} %lengths_ref.5, bf16[2,512,768]{2,1,0:T(8,128)(2,1)} %get-tuple-element.42.x_ref, bf16[9216,768]{1,0:T(8,128)(2,1)} %get-tuple-element.40.table_ref.w_ref, ...), custom_call_target="tpu_custom_call" | custom-call | flops 11274289152 | bytes 18874368 | tf_op jit(solution)/shard_map/attend_back/pallas_call | solution.py:1419
  197.9 0.0 copy-start
  197.9 71.2 %grad_tail.1 = (bf16[1152,768]{1,0:T(8,128)(2,1)}, f32[72,128]{1,0:T(8,128)}, f32[1,1]{1,0:T(1,128)}, bf16[8,128,768]{2,1,0:T(8,128)(2,1)}) custom-call(s32[8]{0:T(128)} %owners_ref.3, bf16[6,2,2,48,768]{4,3,2,1,0:T(8,128)(2,1)} %get-tuple-element.53.qkv_ref, bf16[18,48,768]{2,1,0:T(8,128)(2,1)} %get-tuple-element.54.back_ref, ...), custom_call_target="tpu_custom_call" | custom-call | flops 10000000 | bytes 30000000 | tf_op jit(solution)/shard_map/grad_tail/pallas_call | solution.py:779
  269.8 1.5 multiply_subtract_fusion.1
  271.3 0.0 copy-done
  271.3 0.0 copy-start.1
  271.3 7.5 %multiply_subtract_fusion = (f32[1152,768]{1,0:T(8,128)}, f32[1152,768]{1,0:T(8,128)}, f32[1152,768]{1,0:T(8,128)}) fusion(f32[1152,768]{1,0:T(8,128)S(1)} %copy-done, f32[]{:T(128)S(6)} %min.3, bf16[1152,768]{1,0:T(8,128)(2,1)} %get-tuple-element.59, f32[1152,768]{1,0:T(8,128)} %param.15, f32[1152,768]{1,0:T(8,128)} %param.16), kind=kLoop, calls=%fused_computation.3 | loop fusion | flops 14155776 | bytes 23003140 | tf_op jit(solution)/shard_map/sub | solution.py:54
  278.8 0.0 copy-start.2
  278.8 0.0 copy-done.1
  278.8 1.1 copy.22
  279.9 0.8 copy-done.2
  280.8 1.1 copy.23
Async XLA Ops:
  197.9 73.4 %copy-start = (f32[1152,768]{1,0:T(8,128)S(1)}, f32[1152,768]{1,0:T(8,128)}, u32[]{:S(2)}) copy-start(f32[1152,768]{1,0:T(8,128)} %master_ref.1) | copy-start | bytes 10616836
  271.3 7.5 %copy-start.1 = (bf16[8,128,768]{2,1,0:T(8,128)(2,1)S(1)}, bf16[8,128,768]{2,1,0:T(8,128)(2,1)}, u32[]{:S(2)}) copy-start(bf16[8,128,768]{2,1,0:T(8,128)(2,1)} %get-tuple-element.76) | copy-start | bytes 4718596
  278.8 2.0 copy-start.2
